TPU v7x, 32 devices: a whole 2x2x4 slice. The times are simulated.
32 devices in a mesh: dp: 2 (over y), ctx: 4 (over z), head: 4 (over x, core).
Axes of the slice: x: 2, y: 2, z: 4, core: 2. Of those that a mesh axis runs over, the one named last changes fastest.
Arguments:
- latent: bfloat16 [2, 512, 576], P('dp', 'ctx'), may hold values from -8 to 8
- q_nope: bfloat16 [2, 512, 2048], P('dp', 'ctx', 'head'), may hold values from -6 to 6
- q_rope: bfloat16 [2, 512, 1024], P('dp', 'ctx', 'head'), may hold values from -8 to 8
- grad_out: bfloat16 [2, 512, 2048], P('dp', 'ctx', 'head'), may hold values from -6 to 6
- w_uk: bfloat16 [512, 2048], P(None, 'head'), may hold values from -0.25 to 0.25
- w_uv: bfloat16 [512, 2048], P(None, 'head'), may hold values from -0.25 to 0.25
- stretch_order: int32 [8], replicated, may hold values from 0 to 7, as said below
Outputs:
- d_latent: float32 [2, 512, 576], P('dp', ('ctx', 'head'))
- d_q_nope: bfloat16 [2, 512, 2048], P('dp', 'ctx', 'head')
- d_q_rope: bfloat16 [2, 512, 1024], P('dp', 'ctx', 'head')
- d_w_uk: float32 [512, 2048], P(None, 'head')
- d_w_uv: float32 [512, 2048], P(None, 'head')
Inputs may be any that keep to these rules, and one draw needn't show every extreme that they name: `stretch_order`: entries 2d and 2d+1 name the causal blocks of the two row blocks of the d-th block of 128 rows; all entries together are a permutation, and each such pair sums to 7.
All inputs are finite; a program needn't handle non-finite values.
Results may differ from a plain program's by a relative error of at most 0.02.
Values may be sent and summed in bfloat16 or wider, within the bound.
A program may use at most 64 MiB of HBM per device.

v0:
```python
import math

import jax
import jax.numpy as jnp
from jax import lax
from jax.sharding import PartitionSpec as P

D_LAT = 512
D_ROPE = 64
D_NOPE = 128
D_V = 128
TOK_DEV = 128
STRETCH = 64


NEG_FILL = -1e30


def table_lookup(table, slot_index):
    entries = table.shape[0]
    match = slot_index[:, None] == jnp.arange(entries, dtype=jnp.int32)[None, :]
    return jnp.sum(jnp.where(match, table[None, :], 0), axis=1)


def row_positions(stretch_order, first_row, row_count):
    row_index = first_row + jnp.arange(row_count, dtype=jnp.int32)
    slot_index = 2 * (row_index // TOK_DEV) + row_index % TOK_DEV // STRETCH
    return table_lookup(stretch_order, slot_index) * STRETCH + row_index % STRETCH


def keep_same(current):
    return current


def local(latent, q_nope, q_rope, grad_out, w_uk, w_uv, stretch_order):
    head_count = w_uk.shape[1] // D_NOPE
    n_head = lax.axis_size("head")
    n_ctx = lax.axis_size("ctx")
    ctx_index = lax.axis_index("ctx")
    score_scale = 1.0 / math.sqrt(D_NOPE + D_ROPE)
    key_width = D_LAT + D_ROPE
    w_key = w_uk.reshape(D_LAT, head_count, D_NOPE)
    w_value = w_uv.reshape(D_LAT, head_count, D_V)
    query_heads = q_nope[0].reshape(TOK_DEV, head_count, D_NOPE)
    rope_heads = q_rope[0].reshape(TOK_DEV, head_count, D_ROPE)
    grad_heads = grad_out[0].reshape(TOK_DEV, head_count, D_V)
    query_latent = jnp.einsum(
        "thd,fhd->htf", query_heads, w_key, preferred_element_type=jnp.float32
    ).astype(jnp.bfloat16)
    query_cat = jnp.concatenate([query_latent, rope_heads.transpose(1, 0, 2)], axis=2)
    grad_latent = jnp.einsum(
        "thd,fhd->htf", grad_heads, w_value, preferred_element_type=jnp.float32
    ).astype(jnp.bfloat16)

    def halves(values):
        return (
            values.reshape(head_count, 2, STRETCH, values.shape[-1])
            .transpose(1, 0, 2, 3)
            .reshape(2, head_count * STRETCH, values.shape[-1])
        )

    def unhalve(values):
        return (
            values.reshape(2, head_count, STRETCH, values.shape[-1])
            .transpose(1, 0, 2, 3)
            .reshape(head_count, TOK_DEV, values.shape[-1])
        )

    query_rows = halves(query_cat)
    grad_rows = halves(grad_latent)
    local_pos = row_positions(stretch_order, ctx_index * TOK_DEV, TOK_DEV)
    row_pos = jnp.tile(local_pos.reshape(2, 1, STRETCH), (1, head_count, 1)).reshape(
        2, head_count * STRETCH
    )
    row_top = jnp.max(row_pos, axis=1)
    row_count = head_count * STRETCH

    def scores_of(block_index, key_rows, key_pos):
        raw_score = (
            jnp.einsum(
                "rf,kf->rk", query_rows[block_index], key_rows, preferred_element_type=jnp.float32
            )
            * score_scale
        )
        allowed = key_pos[None, :] <= row_pos[block_index][:, None]
        prob_grad = jnp.einsum(
            "rf,kf->rk",
            grad_rows[block_index],
            key_rows[:, :D_LAT],
            preferred_element_type=jnp.float32,
        )
        return (jnp.where(allowed, raw_score, -jnp.inf), prob_grad)

    stats_init = (
        jnp.full((2, row_count), NEG_FILL, jnp.float32),
        jnp.zeros((2, row_count), jnp.float32),
        jnp.zeros((2, row_count), jnp.float32),
    )
    running = stats_init
    key_rows = lax.all_gather(latent, "ctx", axis=1, tiled=True)[0]
    key_pos = row_positions(stretch_order, jnp.int32(0), key_rows.shape[0])
    for block_index in range(2):

        def stats_update(current, block_index=block_index):
            row_max, row_total, weighted = current
            raw_score, prob_grad = scores_of(block_index, key_rows, key_pos)
            old_max = row_max[block_index]
            new_max = jnp.maximum(old_max, jnp.max(raw_score, axis=1))
            shrink = jnp.exp(old_max - new_max)
            expo = jnp.exp(raw_score - new_max[:, None])
            new_total = row_total[block_index] * shrink + jnp.sum(expo, axis=1)
            new_weighted = weighted[block_index] * shrink + jnp.sum(expo * prob_grad, axis=1)
            return (
                row_max.at[block_index].set(new_max),
                row_total.at[block_index].set(new_total),
                weighted.at[block_index].set(new_weighted),
            )

        needed = jnp.min(key_pos) <= row_top[block_index]
        running = lax.cond(needed, stats_update, keep_same, running)
    row_max, row_total, weighted = running
    log_total = row_max + jnp.log(row_total)
    row_delta = weighted / row_total
    grad_init = (
        jnp.zeros((2, row_count, key_width), jnp.float32),
        jnp.zeros((2, row_count, D_LAT), jnp.float32),
        jnp.zeros((TOK_DEV * n_ctx, key_width), jnp.float32),
    )
    running = grad_init
    grad_key_rows = lax.all_gather(latent, "ctx", axis=1, tiled=True)[0]
    key_count = grad_key_rows.shape[0]
    grad_key_pos = row_positions(stretch_order, jnp.int32(0), key_count)
    for block_index in range(2):

        def grad_update(current, block_index=block_index):
            query_sum, output_sum, latent_sum = current
            raw_score, prob_grad = scores_of(block_index, grad_key_rows, grad_key_pos)
            probability = jnp.exp(raw_score - log_total[block_index][:, None])
            score_grad = (
                score_scale * probability * (prob_grad - row_delta[block_index][:, None])
            ).astype(jnp.bfloat16)
            prob_low = probability.astype(jnp.bfloat16)
            query_sum = query_sum.at[block_index].add(
                jnp.dot(score_grad, grad_key_rows, preferred_element_type=jnp.float32)
            )
            output_sum = output_sum.at[block_index].add(
                jnp.dot(prob_low, grad_key_rows[:, :D_LAT], preferred_element_type=jnp.float32)
            )
            key_term = jnp.einsum(
                "rk,rf->kf", score_grad, query_rows[block_index], preferred_element_type=jnp.float32
            )
            value_term = jnp.einsum(
                "rk,rf->kf", prob_low, grad_rows[block_index], preferred_element_type=jnp.float32
            )
            key_term = key_term.at[:, :D_LAT].add(value_term)
            previous = latent_sum
            latent_sum = previous + key_term
            return (query_sum, output_sum, latent_sum)

        needed = jnp.min(grad_key_pos) <= row_top[block_index]
        running = lax.cond(needed, grad_update, keep_same, running)
    query_sum, output_sum, latent_sum = running
    query_low = unhalve(query_sum.astype(jnp.bfloat16))
    latent_query = query_low[:, :, :D_LAT]
    rope_grad = query_low[:, :, D_LAT:].transpose(1, 0, 2).reshape(1, TOK_DEV, head_count * D_ROPE)
    nope_grad = jnp.einsum("htf,fhd->thd", latent_query, w_key, preferred_element_type=jnp.float32)
    nope_grad = nope_grad.astype(jnp.bfloat16).reshape(1, TOK_DEV, head_count * D_NOPE)
    output_low = unhalve(output_sum.astype(jnp.bfloat16))
    key_weight = jnp.einsum(
        "htf,thd->fhd", latent_query, query_heads, preferred_element_type=jnp.float32
    ).reshape(D_LAT, head_count * D_NOPE)
    value_weight = jnp.einsum(
        "htf,thd->fhd", output_low, grad_heads, preferred_element_type=jnp.float32
    ).reshape(D_LAT, head_count * D_V)
    key_weight, value_weight = lax.psum((key_weight, value_weight), ("dp", "ctx"))
    rows_out = TOK_DEV // n_head
    owner_rows = lax.psum_scatter(
        latent_sum.astype(jnp.bfloat16), "ctx", scatter_dimension=0, tiled=True
    ).astype(jnp.float32)
    owned_rows = lax.psum_scatter(owner_rows, "head", scatter_dimension=0, tiled=True)
    return (
        owned_rows.reshape(1, rows_out, key_width),
        nope_grad,
        rope_grad,
        key_weight,
        value_weight,
    )


def solution(mesh):
    placed = (
        P("dp", "ctx", None),
        P("dp", "ctx", "head"),
        P("dp", "ctx", "head"),
        P("dp", "ctx", "head"),
        P(None, "head"),
        P(None, "head"),
        P(),
    )
    return jax.shard_map(
        local,
        mesh=mesh,
        in_specs=placed,
        out_specs=(
            P("dp", ("ctx", "head"), None),
            P("dp", "ctx", "head"),
            P("dp", "ctx", "head"),
            P(None, "head"),
            P(None, "head"),
        ),
        check_vma=False,
    )
```

profile of v0, /device:TPU:0, one launch (start us, length us, event | category | flops | bytes accessed | tf_op | source)
XLA Modules:
  0.0 200.8 jit_solution(4605810044559342020)
XLA Ops:
  8.1 0.8 select_reduce_fusion.1
  9.1 0.6 fusion.88
  9.7 0.7 select_reduce_fusion
  10.5 0.6 fusion.83
  13.8 0.9 copy.93
  14.9 1.0 copy.116
  15.9 1.1 copy.118
  17.0 1.1 copy.96
  18.1 19.6 %all_gather.4 = bf16[1,512,576]{2,1,0:T(8,128)(2,1)S(1)} all-gather(bf16[1,128,576]{2,1,0:T(8,128)(2,1)S(1)} %copy.96), channel_id=1, replica_groups=mesh['dp'=2,'ctx'=4,'head'=4] {'ctx'}, dimensions={1}, use_global_device_ids=true | all-gather | bytes 737280 | tf_op jit(solution)/shard_map/all_gather | solution.py:130
  38.2 0.6 copy-done.17
  39.9 1.2 conditional.4
  39.9 0.5 fusion.85
  40.4 0.4 fusion.1
  41.1 1.3 conditional.5
  41.1 0.5 fusion.86
  41.7 0.4 fusion.53
  42.5 7.4 %conditional.6 = (f32[2,256,576]{1,2,0:T(8,128)S(1)}, f32[2,256,512]{2,1,0:T(8,128)}, f32[512,576]{0,1:T(8,128)S(1)}) conditional(s32[]{:T(128)} %convert_element_type.45, () %tuple.106, (s32[512]{0:T(512)S(1)}, s32[2,256]{1,0:T(2,128)S(1)}, bf16[2,256,576]{2,1,0:T(8,128)(2,1)S(1)}, bf16[512,576]{1,0:T(8,128)(2,1)S(1)}, f32[2,256]{1,0:T(2,128)S(1)}, ...), branch_computations={%region_14.15_spmd, %region_15.17_spmd} | conditional | flops 857473024 | bytes 30092460 | solution.py:161
  42.5 0.8 compare_reduce_fusion
  43.3 0.5 fusion.13
  44.1 1.4 fusion.18
  45.5 1.0 fusion.10
  46.8 0.4 convolution_bitcast_fusion
  47.5 1.1 scatter-add.6
  48.7 1.2 copy-done.2
  49.9 7.4 %conditional.7 = ((f32[2,256,576]{1,2,0:T(8,128)S(1)}, f32[2,256,512]{2,1,0:T(8,128)}, f32[512,576]{0,1:T(8,128)S(1)})) conditional(s32[]{:T(128)} %convert_element_type.44, (f32[2,256,576]{1,2,0:T(8,128)S(1)}, f32[2,256,512]{2,1,0:T(8,128)}, f32[512,576]{0,1:T(8,128)S(1)}) %conditional.6, (f32[2,256,576]{1,2,0:T(8,128)S(1)}, s32[512]{0:T(512)S(1)}, ...), branch_computations={%region_17.18_spmd, %region_18.20_spmd} | conditional | flops 858046464 | bytes 19868762 | solution.py:161
  49.9 0.6 compare_reduce_fusion.1
  50.5 1.4 fusion.32
  52.0 2.2 %fusion.37 = f32[2,256,512]{2,1,0:T(8,128)} fusion(f32[2,256,512]{2,1,0:T(8,128)} %get-tuple-element.294, bf16[512,576]{1,0:T(8,128)(2,1)S(1)} %get-tuple-element.290, f32[256,512]{1,0:T(8,128)S(1)} %fusion.32), kind=kOutput, calls=%fused_computation.53 | convolution fusion | flops 134479872 | bytes 2097152 | tf_op jit(solution)/shard_map/cond/branch_1_fun/dot_general | solution.py:147
  54.5 0.5 fusion.35
  55.0 0.6 copy-done.5
  56.0 1.0 fusion.29
  57.4 1.1 copy.112
  58.5 22.6 %reduce-scatter.7.cloned.1.call-done = bf16[128,576]{1,0:T(8,128)(2,1)} async-done(((bf16[512,576]{1,0:T(8,128)(2,1)}), bf16[128,576]{1,0:T(8,128)(2,1)}) %reduce-scatter.7.cloned.1.call-update) | async-done | bytes 147472
  81.1 1.1 copy.113
  82.2 0.9 copy.114
  83.1 1.3 convert_element_type.53
  84.8 1.3 copy.108
  86.5 0.5 copy-done.13
  87.3 1.3 copy.105
  88.6 1.0 copy-done.11
  90.0 0.8 copy.110
  90.9 0.7 copy.111
  91.6 11.3 %reduce-scatter.9.cloned.1.call-done = f32[32,576]{1,0:T(8,128)} async-done(((f32[128,576]{1,0:T(8,128)}), f32[32,576]{1,0:T(8,128)}) %reduce-scatter.9.cloned.1.call-update) | async-done | bytes 73744
  103.0 1.0 copy.115
  104.0 0.8 copy.109
  104.8 85.3 %all-reduce.8.cloned.1.call-done = (f32[512,512]{1,0:T(8,128)}, f32[512,512]{1,0:T(8,128)}) async-done(((f32[512,512]{1,0:T(8,128)}, f32[512,512]{1,0:T(8,128)}), (f32[512,512]{1,0:T(8,128)}, f32[512,512]{1,0:T(8,128)})) %all-reduce.8.cloned.1.call-update) | async-done | bytes 2097168 | tf_op jit(solution)/shard_map/psum | solution.py:175
  190.1 2.4 %copy.157 = f32[512,512]{1,0:T(8,128)} copy(f32[512,512]{1,0:T(8,128)} %get-tuple-element.418) | data formatting | bytes 2097152
  192.4 1.0 copy.158
  (90 shorter events, 6.3 us)
Async XLA Ops:
  8.0 29.7 %copy-start = (bf16[512,512]{1,0:T(8,128)(2,1)S(1)}, bf16[512,512]{1,0:T(8,128)(2,1)}, u32[]{:S(2)}) copy-start(bf16[512,512]{1,0:T(8,128)(2,1)} %param.44) | copy-start | bytes 1572868
  8.0 73.1 %reduce-scatter.7.cloned.1.call-start = ((), (), s32[]{:S(2)}) async-start(), calls=%async_computation.2 | async-start | bytes 819200
  15.9 23.1 %copy-start.12 = (bf16[1,128,512]{1,2,0:T(8,128)(2,1)}, bf16[1,128,512]{1,2,0:T(8,128)(2,1)S(1)}, u32[]{:S(2)}) copy-start(bf16[1,128,512]{1,2,0:T(8,128)(2,1)S(1)} %copy.116) | copy-start | bytes 393220
  17.0 21.1 %copy-start.14 = (bf16[1,128,512]{1,2,0:T(8,128)(2,1)}, bf16[1,128,512]{1,2,0:T(8,128)(2,1)S(1)}, u32[]{:S(2)}) copy-start(bf16[1,128,512]{1,2,0:T(8,128)(2,1)S(1)} %copy.118) | copy-start | bytes 393220
  37.7 1.0 copy-start.17
  38.8 3.7 %copy-start.6 = (bf16[2,4,64,512]{3,2,1,0:T(8,128)(2,1)}, bf16[2,4,64,512]{3,2,1,0:T(8,128)(2,1)S(1)}, u32[]{:S(2)}) copy-start(bf16[2,4,64,512]{3,2,1,0:T(8,128)(2,1)S(1)} %copy.99) | copy-start | bytes 1572868
  39.0 0.8 copy-start.10
  39.9 2.6 %copy-start.3 = (bf16[2,4,64,576]{3,2,1,0:T(8,128)(2,1)}, bf16[2,4,64,576]{3,2,1,0:T(8,128)(2,1)S(1)}, u32[]{:S(2)}) copy-start(bf16[2,4,64,576]{3,2,1,0:T(8,128)(2,1)S(1)} %copy.95) | copy-start | bytes 1769476
  42.5 1.2 copy-start.4
  42.5 1.2 copy-start.7
  44.1 1.4 copy-start.8
  46.5 1.0 copy-start.1
  48.6 1.3 copy-start.2
  52.0 2.2 %copy-start.9 = (bf16[2,256,512]{2,1,0:T(8,128)(2,1)S(1)}, bf16[2,256,512]{2,1,0:T(8,128)(2,1)}, u32[]{:S(2)}) copy-start(bf16[2,256,512]{2,1,0:T(8,128)(2,1)} %get-tuple-element.292) | copy-start | bytes 1572868 | tf_op jit(solution)/shard_map/cond
  54.5 1.1 copy-start.5
  58.5 44.5 %reduce-scatter.9.cloned.1.call-start = ((), (), s32[]{:S(2)}) async-start(), calls=%async_computation.3 | async-start | bytes 409600
  83.1 107.0 %all-reduce.8.cloned.1.call-start = ((), (), s32[]{:S(2)}) async-start(), calls=%async_computation.4 | async-start | bytes 4194304 | tf_op jit(solution)/shard_map/psum | solution.py:175
  83.1 1.4 copy-start.15
  86.1 0.9 copy-start.13
  88.6 1.1 copy-start.11
  190.1 2.4 %copy-start.16 = (f32[512,512]{1,0:T(8,128)S(1)}, f32[512,512]{1,0:T(8,128)}, u32[]{:S(2)}) copy-start(f32[512,512]{1,0:T(8,128)} %get-tuple-element.419) | copy-start | bytes 3145732
Sparse Core Ops, SparseCore 0:
  58.6 22.4 reduce-scatter.6
  83.6 19.3 reduce-scatter.8
Sparse Core Ops, SparseCore 1:
  88.7 101.3 all-reduce.7
where the time goes:
time: 202 us; the launch traced here: 201 us
  waiting for transfers between devices  119 us (59%)
  local copies, waits for them, and re-layouts  24.2 us (12%)
  blocking collectives  19.6 us (10%)
  between operations  18.3 us (9%)
  matrix products  13 us (6%)
  other arithmetic  6.04 us (3%)
    psum x1, waiting for transfers between devices, local(): lax.psum((key_weight, value_weight), ('dp', 'ctx'))  85.3 us
    unnamed x5, waiting for transfers between devices  33.9 us
    all_gather x1, blocking collectives, local(): grad_key_rows = lax.all_gather(latent, 'ctx', axis=1, tiled=True)[0]  19.6 us
    unnamed x33, local copies, waits for them, and re-layouts  14.3 us
  transfers between devices with their start and end apart: 3, of which 3 were waited for; matrix products, arithmetic and copies ran while one was open for 4% of the time, Pallas kernels for 0%

commit v1 on v0

v1 whole, which is shorter than its diff:
```python
import functools
import math

import jax
import jax.numpy as jnp
from jax import lax
from jax.experimental import pallas as pl
from jax.experimental.pallas import tpu as pltpu
from jax.sharding import PartitionSpec as P

D_LAT = 512
D_ROPE = 64
D_NOPE = 128
D_V = 128
TOK = 128
STRETCH = 64
WIDTH = D_LAT + D_ROPE
SCALE = 1.0 / math.sqrt(D_NOPE + D_ROPE)
MESH = pl.DeviceIdType.MESH
BF16 = jnp.bfloat16
F32 = jnp.float32


def dot_nn(a, b):
    return jnp.dot(a, b, preferred_element_type=F32)


def dot_nt(a, b):
    return lax.dot_general(a, b, (((1,), (1,)), ((), ())), preferred_element_type=F32)


def dot_tn(a, b):
    return lax.dot_general(a, b, (((0,), (0,)), ((), ())), preferred_element_type=F32)


def body(
    n_ctx, n_head, heads,
    lat, qn, qr, g, wk, wv, order,
    d_lat, d_qn, d_qr, d_wk, d_wv,
    gath, qc, gl, ql, key_pos, row_pos, pb, ds,
    wpart, yown, yrecv, zsend, zrecv, own, final, gsend, hrecv, lsend, lrecv,
    lat_s, lat_r, fwd_s, fwd_r, y_s, y_r, z_s, z_r, ag_s, ag_r, yag_s, yag_r, h_s, h_r, l_s, l_r,
    yown_s, zown_s, own_s, hown_s,
):
    rep = lax.axis_index("dp")
    ctx = lax.axis_index("ctx")
    head = lax.axis_index("head")
    other = 1 - rep
    half = lax.rem(head, 2)
    sibling = head + 1 - 2 * half

    def ctx_at(step):
        return lax.rem(ctx + step + n_ctx, n_ctx)

    def head_at(step):
        return lax.rem(head + step + n_head, n_head)

    def copy(src, dst, send, recv, target):
        return pltpu.make_async_remote_copy(
            src_ref=src, dst_ref=dst, send_sem=send, recv_sem=recv,
            device_id=target, device_id_type=MESH,
        )

    partners = [(rep, ctx_at(k), head) for k in range(1, n_ctx)]
    partners += [(rep, ctx, head_at(k)) for k in range(1, n_head)]
    partners += [(other, ctx, head)]
    barrier = pltpu.get_barrier_semaphore()
    for target in partners:
        pl.semaphore_signal(barrier, inc=1, device_id=target, device_id_type=MESH)
    pl.semaphore_wait(barrier, len(partners))

    sends = []

    def start(c):
        c.start()
        sends.append(c)
        return c

    def keep(src, dst, sem):
        c = pltpu.make_async_copy(src, dst, sem)
        c.start()
        return c

    lat_copies = [
        start(copy(lat.at[half], gath.at[k, half], lat_s.at[k - 1], lat_r.at[k - 1],
                   (rep, ctx_at(k), head)))
        for k in range(1, n_ctx)
    ]
    gath[0] = lat[...]

    def each(count, step):
        def run(i, carry):
            step(i)
            return carry

        lax.fori_loop(0, count, run, 0)

    def tile(m):
        return pl.ds(pl.multiple_of(m * 128, 128), 128)

    def project(m):
        rows = tile(m)
        qc[rows, :D_LAT] = dot_nt(qn[0, :, rows], wk[:, rows]).astype(BF16)
        gl[rows, :] = dot_nt(g[0, :, rows], wv[:, rows]).astype(BF16)

    each(heads, project)
    for m in range(heads):
        qc[m * TOK:(m + 1) * TOK, D_LAT:] = qr[0, :, m * D_ROPE:(m + 1) * D_ROPE]

    fwd_copies = []
    for k in range(1, n_ctx):
        lat_copies[k - 1].wait_recv()
        fwd_copies.append(
            start(copy(gath.at[k, half], gath.at[k, half], fwd_s.at[k - 1], fwd_r.at[k - 1],
                       (rep, ctx, sibling))))

    n_keys = n_ctx * TOK
    lane = lax.broadcasted_iota(jnp.int32, (1, n_keys), 1)
    start_pos = jnp.zeros((1, n_keys), jnp.int32)
    for k in range(n_ctx):
        owner = ctx_at(-k)
        for part in range(2):
            first = k * TOK + part * STRETCH
            inside = (lane >= first) & (lane < first + STRETCH)
            start_pos = start_pos + jnp.where(inside, order[2 * owner + part] * STRETCH, 0)
    key_pos[...] = start_pos + lane % STRETCH
    row = lax.broadcasted_iota(jnp.int32, (TOK, 1), 0)
    row_start = jnp.where(row < STRETCH, order[2 * ctx], order[2 * ctx + 1]) * STRETCH
    row_pos[...] = row_start + row % STRETCH

    for k in range(1, n_ctx):
        fwd_copies[k - 1].wait_recv()

    part_rows = wpart.shape[3]

    def weight_term(which, low, value, cols):
        term = dot_tn(low, value[0, :, cols]).astype(BF16)
        wpart[which, :, :, :, cols] = term.reshape(2, n_ctx, part_rows, 128)

    def send_half(which):
        return (
            keep(wpart.at[which, rep], yown.at[which], yown_s.at[which]),
            start(copy(wpart.at[which, other], yrecv.at[which], y_s.at[which], y_r.at[which],
                       (other, ctx, head))),
        )

    def attend(m):
        rows = tile(m)
        keys = gath[...].reshape(n_keys, WIDTH)
        score = dot_nt(qc[rows, :], keys) * SCALE
        score = jnp.where(key_pos[...] <= row_pos[...], score, -jnp.inf)
        expo = jnp.exp(score - jnp.max(score, axis=1, keepdims=True))
        prob = expo * (1.0 / jnp.sum(expo, axis=1, keepdims=True))
        low = prob.astype(BF16)
        pb[rows, :] = low
        grad = dot_nt(gl[rows, :], keys[:, :D_LAT])
        delta = jnp.sum(prob * grad, axis=1, keepdims=True)
        ds[rows, :] = (SCALE * prob * (grad - delta)).astype(BF16)
        out_low = dot_nn(low, keys[:, :D_LAT]).astype(BF16)
        weight_term(0, out_low, g, rows)

    each(heads, attend)
    y_copies = [send_half(0)]

    def query_side(m):
        rows = tile(m)
        keys = gath[...].reshape(n_keys, WIDTH)
        low = dot_nn(ds[rows, :], keys).astype(BF16)
        ql[rows, :] = low
        weight_term(1, low[:, :D_LAT], qn, rows)

    each(heads, query_side)
    y_copies.append(send_half(1))

    own_rows = TOK // n_head

    def key_side(k):
        cols = tile(k)
        value = dot_tn(pb[:, cols], gl[...])
        key = dot_tn(ds[:, cols], qc[...])
        low = key[:, :D_LAT] + value
        gsend[:, k, :, :D_LAT] = low.reshape(n_head, own_rows, D_LAT).astype(BF16)
        gsend[:, k, :, D_LAT:] = key[:, D_LAT:].reshape(n_head, own_rows, D_ROPE).astype(BF16)

    each(n_ctx, key_side)
    h_own = keep(gsend.at[head], hrecv.at[n_head - 1], hown_s.at[0])
    h_copies = [
        start(copy(gsend.at[head_at(k)], hrecv.at[k - 1], h_s.at[k - 1], h_r.at[k - 1],
                   (rep, ctx, head_at(k))))
        for k in range(1, n_head)
    ]

    def spread(which):
        y_copies[which][0].wait()
        y_copies[which][1].wait_recv()

        def add(i):
            total = yown[which, i].astype(F32) + yrecv[which, i].astype(F32)
            zsend[which, i] = total.astype(BF16)

        each(n_ctx, add)
        z_own.append(keep(zsend.at[which, ctx], zrecv.at[which, n_ctx - 1], zown_s.at[which]))
        return [
            start(copy(zsend.at[which, ctx_at(k)], zrecv.at[which, k - 1],
                       z_s.at[which, k - 1], z_r.at[which, k - 1], (rep, ctx_at(k), head)))
            for k in range(1, n_ctx)
        ]

    z_own = []
    z_copies = [spread(0)]

    def nope(m):
        rows = tile(m)
        d_qn[0, :, rows] = dot_nn(ql[rows, :D_LAT], wk[:, rows]).astype(BF16)

    each(heads, nope)
    for m in range(heads):
        d_qr[0, :, m * D_ROPE:(m + 1) * D_ROPE] = ql[m * TOK:(m + 1) * TOK, D_LAT:]
    z_copies.append(spread(1))

    h_own.wait()
    for c in h_copies:
        c.wait_recv()
    l_copies = []
    owned = None
    for k in range(n_ctx):
        total = hrecv[n_head - 1, k].astype(F32)
        for i in range(n_head - 1):
            total = total + hrecv[i, k].astype(F32)
        if k == 0:
            owned = total
        else:
            lsend[k - 1] = total.astype(BF16)
            l_copies.append(
                start(copy(lsend.at[k - 1], lrecv.at[k - 1], l_s.at[k - 1], l_r.at[k - 1],
                           (rep, ctx_at(-k), head))))

    ag_copies, yag_copies, own_copies = [], [], []
    for which in range(2):
        z_own[which].wait()
        for c in z_copies[which]:
            c.wait_recv()
        total = zrecv[which, n_ctx - 1].astype(F32)
        for k in range(1, n_ctx):
            total = total + zrecv[which, k - 1].astype(F32)
        own[which] = total.astype(BF16)
        mine = final.at[which, rep, ctx]
        own_copies.append(keep(own.at[which], mine, own_s.at[which]))
        ag_copies.append([
            start(copy(own.at[which], mine, ag_s.at[which, k - 1], ag_r.at[which, k - 1],
                       (rep, ctx_at(k), head)))
            for k in range(1, n_ctx)
        ])
        yag_copies.append([
            start(copy(own.at[which], mine, yag_s.at[which, 0], yag_r.at[which, 0], (other, ctx, head)))
        ])

    for c in l_copies:
        c.wait_recv()
    for k in range(1, n_ctx):
        owned = owned + lrecv[k - 1].astype(F32)
    d_lat[...] = owned

    for which in range(2):
        for k in range(1, n_ctx):
            there = final.at[which, rep, ctx_at(-k)]
            copy(there, there, ag_s.at[which, k - 1], ag_r.at[which, k - 1],
                 (rep, ctx_at(k), head)).wait_recv()
            yag_copies[which].append(
                start(copy(there, there, yag_s.at[which, k], yag_r.at[which, k],
                           (other, ctx, head))))
    for which, out in ((0, d_wv), (1, d_wk)):
        for k in range(n_ctx):
            there = final.at[which, other, ctx_at(-k)]
            copy(there, there, yag_s.at[which, k], yag_r.at[which, k],
                 (other, ctx, head)).wait_recv()
        own_copies[which].wait()

        def widen(i):
            first = pl.multiple_of(i * part_rows, part_rows)
            low = final[which, i // n_ctx, i % n_ctx]
            out[pl.ds(first, part_rows), :] = low.astype(F32)

        each(2 * n_ctx, widen)
    for c in sends:
        c.wait_send()


def local(n_ctx, n_head, latent, q_nope, q_rope, grad_out, w_uk, w_uv, stretch_order):
    heads = w_uk.shape[1] // D_NOPE
    rows = heads * TOK
    n_keys = n_ctx * TOK
    own = TOK // n_head
    part_rows = D_LAT // (2 * n_ctx)
    cols = w_uk.shape[1]
    vmem = pl.BlockSpec(memory_space=pltpu.VMEM)
    dma = pltpu.SemaphoreType.DMA
    outs = pl.pallas_call(
        functools.partial(body, n_ctx, n_head, heads),
        out_shape=(
            jax.ShapeDtypeStruct((own, WIDTH), F32),
            jax.ShapeDtypeStruct(q_nope.shape, BF16),
            jax.ShapeDtypeStruct(q_rope.shape, BF16),
            jax.ShapeDtypeStruct(w_uk.shape, F32),
            jax.ShapeDtypeStruct(w_uv.shape, F32),
        ),
        in_specs=[vmem] * 6 + [pl.BlockSpec(memory_space=pltpu.SMEM)],
        out_specs=(vmem,) * 5,
        scratch_shapes=[
            pltpu.VMEM((n_ctx, 2, TOK // 2, WIDTH), BF16),
            pltpu.VMEM((rows, WIDTH), BF16),
            pltpu.VMEM((rows, D_LAT), BF16),
            pltpu.VMEM((rows, WIDTH), BF16),
            pltpu.VMEM((1, n_keys), jnp.int32),
            pltpu.VMEM((TOK, 1), jnp.int32),
            pltpu.VMEM((rows, n_keys), BF16),
            pltpu.VMEM((rows, n_keys), BF16),
            pltpu.VMEM((2, 2, n_ctx, part_rows, cols), BF16),
            pltpu.VMEM((2, n_ctx, part_rows, cols), BF16),
            pltpu.VMEM((2, n_ctx, part_rows, cols), BF16),
            pltpu.VMEM((2, n_ctx, part_rows, cols), BF16),
            pltpu.VMEM((2, n_ctx, part_rows, cols), BF16),
            pltpu.VMEM((2, part_rows, cols), BF16),
            pltpu.VMEM((2, 2, n_ctx, part_rows, cols), BF16),
            pltpu.VMEM((n_head, n_ctx, own, WIDTH), BF16),
            pltpu.VMEM((n_head, n_ctx, own, WIDTH), BF16),
            pltpu.VMEM((n_ctx - 1, own, WIDTH), BF16),
            pltpu.VMEM((n_ctx - 1, own, WIDTH), BF16),
            dma((n_ctx - 1,)), dma((n_ctx - 1,)),
            dma((n_ctx - 1,)), dma((n_ctx - 1,)),
            dma((2,)), dma((2,)),
            dma((2, n_ctx - 1)), dma((2, n_ctx - 1)),
            dma((2, n_ctx - 1)), dma((2, n_ctx - 1)),
            dma((2, n_ctx)), dma((2, n_ctx)),
            dma((n_head - 1,)), dma((n_head - 1,)),
            dma((n_ctx - 1,)), dma((n_ctx - 1,)),
            dma((2,)), dma((2,)), dma((2,)), dma((1,)),
        ],
        compiler_params=pltpu.CompilerParams(
            collective_id=0, has_side_effects=True, vmem_limit_bytes=56 << 20
        ),
    )(latent.reshape(2, TOK // 2, WIDTH), q_nope, q_rope, grad_out, w_uk, w_uv, stretch_order)
    return (outs[0][None],) + tuple(outs[1:])


def solution(mesh):
    n_ctx, n_head = mesh.shape["ctx"], mesh.shape["head"]
    placed = (
        P("dp", "ctx", None),
        P("dp", "ctx", "head"),
        P("dp", "ctx", "head"),
        P("dp", "ctx", "head"),
        P(None, "head"),
        P(None, "head"),
        P(),
    )
    return jax.shard_map(
        functools.partial(local, n_ctx, n_head),
        mesh=mesh,
        in_specs=placed,
        out_specs=(
            P("dp", ("ctx", "head"), None),
            P("dp", "ctx", "head"),
            P("dp", "ctx", "head"),
            P(None, "head"),
            P(None, "head"),
        ),
        check_vma=False,
    )
```

time: 202 us -> 70.6 us (0.35)
  waiting for transfers between devices: 119 us -> 0 us
  Pallas kernels: 0 us -> 61.6 us
  blocking collectives: 19.6 us -> 0 us
  between operations: 18.3 us -> 0.65 us
  local copies, waits for them, and re-layouts: 24.2 us -> 8.1 us
  matrix products: 13 us -> 0 us
  other arithmetic: 6.04 us -> 0 us
    psum x1 -> x0, waiting for transfers between devices: 85.3 us -> none  [local(): lax.psum((key_weight, value_weight), ('dp', 'ctx'))]
    pallas_call x0 -> x1, Pallas kernels: none -> 61.6 us  [local(): pl.pallas_call(functools.partial(body, n_ctx, n_head, heads), out_shape=(...]
    unnamed x5 -> x0, waiting for transfers between devices: 33.9 us -> none
    all_gather x1 -> x0, blocking collectives: 19.6 us -> none  [local(): grad_key_rows = lax.all_gather(latent, 'ctx', axis=1, tiled=True)[0]]
    dot_general x21 -> x0, matrix products: 13 us -> none  [the longest x4 2.86 us: scores_of(): jnp.einsum('rf,kf->rk', query_rows[block_index], key_rows, preferred_elem...]
    unnamed x33 -> x12, local copies, waits for them, and re-layouts: 14.3 us -> 8.1 us
    reshape x3 -> x0, local copies, waits for them, and re-layouts: 2.83 us -> none  [the longest x1 1.31 us: local(): value_weight = jnp.einsum('htf,thd->fhd', output_low, grad_heads, preferr...]
    cond x15 -> x0, local copies, waits for them, and re-layouts: 2.38 us -> none
  transfers between devices with their start and end apart: 3 -> 0, of which waited for: 3 -> 0; matrix products, arithmetic and copies ran while one was open for 4% -> 0% of each run, Pallas kernels for 0% -> 0%
where the time goes in v1:
time: 70.6 us; the launch traced here: 70.3 us
  Pallas kernels  61.6 us (87%)
  local copies, waits for them, and re-layouts  8.1 us (11%)
    pallas_call x1, Pallas kernels, local(): pl.pallas_call(functools.partial(body, n_ctx, n_head, heads), out_shape=(...  61.6 us
    unnamed x12, local copies, waits for them, and re-layouts  8.1 us

profile of v1, /device:TPU:0, one launch (start us, length us, event | category | flops | bytes accessed | tf_op | source)
XLA Modules:
  0.0 70.3 jit_solution(14677273514817581096)
XLA Ops:
  0.6 1.7 %copy.12 = bf16[1,128,576]{2,1,0:T(8,128)(2,1)} copy(bf16[1,128,576]{1,2,0:T(8,128)(2,1)} %param.7) | data formatting | bytes 294912 | tf_op args[0]
  2.3 61.6 %shard_map.110 = (f32[32,576]{1,0:T(8,128)}, bf16[1,128,512]{2,1,0:T(8,128)(2,1)}, bf16[1,128,256]{2,1,0:T(8,128)(2,1)}, f32[512,512]{1,0:T(8,128)}, f32[512,512]{1,0:T(8,128)}) custom-call(bf16[2,64,576]{2,1,0:T(8,128)(2,1)} %bitcast.2, bf16[1,128,512]{2,1,0:T(8,128)(2,1)} %qn.1, bf16[1,128,256]{2,1,0:T(8,128)(2,1)} %qr.1, bf16[1,128,512]{2,1,0:T(8,128)(2,1)} %g.1, ...), custom_call_target="tpu_custom_call" | custom-call | tf_op jit(solution)/shard_map/pallas_call | solution.py:298
  63.9 0.0 copy-start.1
  63.9 1.6 %copy.18 = f32[1,32,576]{2,1,0:T(8,128)} copy(f32[1,32,576]{2,1,0:T(8,128)} %bitcast.3) | data formatting | bytes 147456
  65.5 0.0 copy-done.1
  65.5 0.0 copy-start.2
  65.5 0.7 copy.19
  66.1 0.2 copy-done.2
  66.3 0.6 copy.20
  67.0 0.0 copy-start
  67.0 2.4 %copy.21 = f32[512,512]{1,0:T(8,128)} copy(f32[512,512]{1,0:T(8,128)} %get-tuple-element.23) | data formatting | bytes 2097152
  69.3 0.0 copy-done
  69.3 1.0 %copy.22 = f32[512,512]{1,0:T(8,128)} copy(f32[512,512]{1,0:T(8,128)S(1)} %copy-done) | data formatting | bytes 2097152
Async XLA Ops:
  63.9 1.6 %copy-start.1 = (bf16[1,128,512]{2,1,0:T(8,128)(2,1)S(1)}, bf16[1,128,512]{2,1,0:T(8,128)(2,1)}, u32[]{:S(2)}) copy-start(bf16[1,128,512]{2,1,0:T(8,128)(2,1)} %get-tuple-element.21) | copy-start | bytes 393220
  65.5 0.9 %copy-start.2 = (bf16[1,128,256]{2,1,0:T(8,128)(2,1)S(1)}, bf16[1,128,256]{2,1,0:T(8,128)(2,1)}, u32[]{:S(2)}) copy-start(bf16[1,128,256]{2,1,0:T(8,128)(2,1)} %get-tuple-element.22) | copy-start | bytes 196612
  67.0 2.4 %copy-start = (f32[512,512]{1,0:T(8,128)S(1)}, f32[512,512]{1,0:T(8,128)}, u32[]{:S(2)}) copy-start(f32[512,512]{1,0:T(8,128)} %get-tuple-element.24) | copy-start | bytes 3145732

commit v2 on v1

v2 whole, which is shorter than its diff:
```python
import functools
import math

import jax
import jax.numpy as jnp
from jax import lax
from jax.experimental import pallas as pl
from jax.experimental.pallas import tpu as pltpu
from jax.sharding import PartitionSpec as P

D_LAT = 512
D_ROPE = 64
D_NOPE = 128
D_V = 128
TOK = 128
STRETCH = 64
PAIR = 2
WIDTH = D_LAT + D_ROPE
SCALE = 1.0 / math.sqrt(D_NOPE + D_ROPE)
MESH = pl.DeviceIdType.MESH
BF16 = jnp.bfloat16
F32 = jnp.float32


def dot_nn(a, b):
    return jnp.dot(a, b, preferred_element_type=F32)


def dot_nt(a, b):
    return lax.dot_general(a, b, (((1,), (1,)), ((), ())), preferred_element_type=F32)


def dot_tn(a, b):
    return lax.dot_general(a, b, (((0,), (0,)), ((), ())), preferred_element_type=F32)


def body(
    n_ctx, n_head, groups,
    lat, qn, qr, g, wk, wv, order,
    d_lat, d_qn, d_qr, final,
    gath, qc, gl, ql, key_pos, row_pos, pb, ds,
    wpart, yown, yrecv, zsend, zrecv, own, gsend, hrecv, lsend, lrecv,
    lat_s, lat_r, fwd_s, fwd_r, y_s, y_r, z_s, z_r, ag_s, ag_r, yag_s, yag_r, h_s, h_r, l_s, l_r,
    yown_s, zown_s, own_s, hown_s,
):
    rep = lax.axis_index("dp")
    ctx = lax.axis_index("ctx")
    head = lax.axis_index("head")
    other = 1 - rep
    half = lax.rem(head, 2)
    sibling = head + 1 - 2 * half
    pieces = 2 * groups
    part_rows = own.shape[1]
    n_keys = n_ctx * TOK
    ctx_steps = range(1, n_ctx)

    def ctx_at(step):
        return lax.rem(ctx + step + n_ctx, n_ctx)

    def head_at(step):
        return lax.rem(head + step + n_head, n_head)

    def copy(src, dst, send, recv, target):
        return pltpu.make_async_remote_copy(
            src_ref=src, dst_ref=dst, send_sem=send, recv_sem=recv,
            device_id=target, device_id_type=MESH,
        )

    def each(first, last, step):
        def run(i, carry):
            step(i)
            return carry

        lax.fori_loop(first, last, run, 0)

    def tile(m, size):
        return pl.ds(pl.multiple_of(m * size, size), size)

    def lat_copy(k):
        cols = slice(k * TOK, (k + 1) * TOK)
        return copy(lat.at[half], gath.at[half, :, cols], lat_s.at[k - 1], lat_r.at[k - 1],
                    (rep, ctx_at(k), head))

    def fwd_copy(k):
        block = gath.at[half, :, slice(k * TOK, (k + 1) * TOK)]
        return copy(block, block, fwd_s.at[k - 1], fwd_r.at[k - 1], (rep, ctx, sibling))

    def y_copy(p):
        return copy(wpart.at[p, other], yrecv.at[p], y_s.at[p], y_r.at[p], (other, ctx, head))

    def y_keep(p):
        return pltpu.make_async_copy(wpart.at[p, rep], yown.at[p], yown_s.at[p])

    def z_copy(p, k):
        return copy(zsend.at[p, ctx_at(k)], zrecv.at[p, k - 1], z_s.at[p, k - 1], z_r.at[p, k - 1],
                    (rep, ctx_at(k), head))

    def z_keep(p):
        return pltpu.make_async_copy(zsend.at[p, ctx], zrecv.at[p, n_ctx - 1], zown_s.at[p])

    def ag_copy(p, k):
        return copy(own.at[p], final.at[p, rep, ctx], ag_s.at[p, k - 1], ag_r.at[p, k - 1],
                    (rep, ctx_at(k), head))

    def own_keep(p):
        return pltpu.make_async_copy(own.at[p], final.at[p, rep, ctx], own_s.at[p])

    def yag_copy(p, k):
        there = final.at[p, rep, ctx_at(-k)]
        return copy(own.at[p] if k == 0 else there, there, yag_s.at[p, k], yag_r.at[p, k],
                    (other, ctx, head))

    def h_copy(k):
        return copy(gsend.at[head_at(k)], hrecv.at[k - 1], h_s.at[k - 1], h_r.at[k - 1],
                    (rep, ctx, head_at(k)))

    def l_copy(k):
        return copy(lsend.at[k - 1], lrecv.at[k - 1], l_s.at[k - 1], l_r.at[k - 1],
                    (rep, ctx_at(-k), head))

    partners = [(rep, ctx_at(k), head) for k in ctx_steps]
    partners += [(rep, ctx, head_at(k)) for k in range(1, n_head)]
    partners += [(other, ctx, head)]
    barrier = pltpu.get_barrier_semaphore()
    for target in partners:
        pl.semaphore_signal(barrier, inc=1, device_id=target, device_id_type=MESH)
    pl.semaphore_wait(barrier, len(partners))

    for k in ctx_steps:
        lat_copy(k).start()
    gath[:, :, :TOK] = lat[...]

    def project(i):
        for sub in range(PAIR):
            rows = tile(i * PAIR + sub, 128)
            qc[rows, :D_LAT] = dot_nt(qn[0, :, rows], wk[:, rows]).astype(BF16)
            gl[rows, :] = dot_nt(g[0, :, rows], wv[:, rows]).astype(BF16)

    each(0, groups, project)
    for m in range(groups * PAIR):
        qc[m * TOK:(m + 1) * TOK, D_LAT:] = qr[0, :, m * D_ROPE:(m + 1) * D_ROPE]

    lane = lax.broadcasted_iota(jnp.int32, (1, n_keys), 1)
    start_pos = jnp.zeros((1, n_keys), jnp.int32)
    for k in range(n_ctx):
        owner = ctx_at(-k)
        for part in range(2):
            first = k * TOK + part * STRETCH
            inside = (lane >= first) & (lane < first + STRETCH)
            start_pos = start_pos + jnp.where(inside, order[2 * owner + part] * STRETCH, 0)
    key_pos[...] = start_pos + lane % STRETCH
    row = lax.broadcasted_iota(jnp.int32, (PAIR * TOK, 1), 0) % TOK
    row_start = jnp.where(row < STRETCH, order[2 * ctx], order[2 * ctx + 1]) * STRETCH
    row_pos[...] = row_start + row % STRETCH

    for k in ctx_steps:
        lat_copy(k).wait_recv()
        fwd_copy(k).start()
    for k in ctx_steps:
        fwd_copy(k).wait_recv()

    def weight_term(p, low, value, i):
        for sub in range(PAIR):
            cols = tile(i * PAIR + sub, 128)
            term = dot_tn(low[sub * TOK:(sub + 1) * TOK, :D_LAT], value[0, :, cols]).astype(BF16)
            wpart[p, :, :, :, sub * 128:(sub + 1) * 128] = term.reshape(2, n_ctx, part_rows, 128)
        y_keep(p).start()
        y_copy(p).start()

    def attend(i):
        rows = tile(i, PAIR * TOK)
        keys = gath[...].reshape(WIDTH, n_keys)
        score = dot_nn(qc[rows, :], keys) * SCALE
        score = jnp.where(key_pos[...] <= row_pos[...], score, -jnp.inf)
        expo = jnp.exp(score - jnp.max(score, axis=1, keepdims=True))
        prob = expo * (1.0 / jnp.sum(expo, axis=1, keepdims=True))
        low = prob.astype(BF16)
        pb[rows, :] = low
        grad = dot_nn(gl[rows, :], keys[:D_LAT, :])
        delta = jnp.sum(prob * grad, axis=1, keepdims=True)
        ds[rows, :] = (SCALE * prob * (grad - delta)).astype(BF16)
        out_low = dot_nt(low, keys[:D_LAT, :]).astype(BF16)
        weight_term(i, out_low, g, i)

    def spread(p):
        y_keep(p).wait()
        y_copy(p).wait_recv()

        def add(i):
            total = yown[p, i].astype(F32) + yrecv[p, i].astype(F32)
            zsend[p, i] = total.astype(BF16)

        each(0, n_ctx, add)
        z_keep(p).start()
        for k in ctx_steps:
            z_copy(p, k).start()

    def query_side(i):
        spread(i)
        rows = tile(i, PAIR * TOK)
        keys = gath[...].reshape(WIDTH, n_keys)
        low = dot_nt(ds[rows, :], keys).astype(BF16)
        ql[rows, :] = low
        weight_term(groups + i, low, qn, i)

    own_rows = TOK // n_head

    def key_side(k):
        cols = tile(k, TOK)
        value = dot_tn(pb[:, cols], gl[...])
        key = dot_tn(ds[:, cols], qc[...])
        low = key[:, :D_LAT] + value
        gsend[:, k, :, :D_LAT] = low.reshape(n_head, own_rows, D_LAT).astype(BF16)
        gsend[:, k, :, D_LAT:] = key[:, D_LAT:].reshape(n_head, own_rows, D_ROPE).astype(BF16)

    each(0, groups, attend)
    each(0, groups, query_side)
    for i in range(groups):
        each(i * n_ctx // groups, (i + 1) * n_ctx // groups, key_side)
        spread(groups + i)
    h_keep = pltpu.make_async_copy(gsend.at[head], hrecv.at[n_head - 1], hown_s.at[0])
    h_keep.start()
    for k in range(1, n_head):
        h_copy(k).start()

    def nope(i):
        for sub in range(PAIR):
            rows = tile(i * PAIR + sub, 128)
            d_qn[0, :, rows] = dot_nn(ql[rows, :D_LAT], wk[:, rows]).astype(BF16)

    each(0, groups, nope)
    for m in range(groups * PAIR):
        d_qr[0, :, m * D_ROPE:(m + 1) * D_ROPE] = ql[m * TOK:(m + 1) * TOK, D_LAT:]

    def settle(p):
        z_keep(p).wait()
        total = zrecv[p, n_ctx - 1].astype(F32)
        for k in ctx_steps:
            z_copy(p, k).wait_recv()
            total = total + zrecv[p, k - 1].astype(F32)
        own[p] = total.astype(BF16)
        for k in ctx_steps:
            ag_copy(p, k).start()
        yag_copy(p, 0).start()
        own_keep(p).start()

    def hand_on(p):
        for k in ctx_steps:
            there = final.at[p, rep, ctx_at(-k)]
            copy(there, there, ag_s.at[p, k - 1], ag_r.at[p, k - 1],
                 (rep, ctx_at(k), head)).wait_recv()
            yag_copy(p, k).start()

    def latent_terms():
        h_keep.wait()
        for k in range(1, n_head):
            h_copy(k).wait_recv()
        for k in range(n_ctx):
            total = hrecv[n_head - 1, k].astype(F32)
            for i in range(n_head - 1):
                total = total + hrecv[i, k].astype(F32)
            if k == 0:
                d_lat[...] = total
            else:
                lsend[k - 1] = total.astype(BF16)
                l_copy(k).start()

    for p in range(groups):
        settle(p)
    latent_terms()
    for p in range(groups):
        settle(groups + p)
        hand_on(p)
    for p in range(groups):
        hand_on(groups + p)
    total = d_lat[...]
    for k in ctx_steps:
        l_copy(k).wait_recv()
        total = total + lrecv[k - 1].astype(F32)
    d_lat[...] = total

    for k in ctx_steps:
        lat_copy(k).wait_send()
        fwd_copy(k).wait_send()
        l_copy(k).wait_send()
    for k in range(1, n_head):
        h_copy(k).wait_send()
    for p in range(pieces):
        y_copy(p).wait_send()
        own_keep(p).wait()
        for k in ctx_steps:
            z_copy(p, k).wait_send()
            ag_copy(p, k).wait_send()
        for k in range(n_ctx):
            there = final.at[p, other, ctx_at(-k)]
            arrived = copy(there, there, yag_s.at[p, k], yag_r.at[p, k], (other, ctx, head))
            arrived.wait_recv()
            yag_copy(p, k).wait_send()


def finish(groups, lat, qn, qr, weights, d_lat, d_qn, d_qr, d_wk, d_wv):
    d_lat[0] = lat[...]
    d_qn[...] = qn[...]
    d_qr[...] = qr[...]
    for which, out in ((0, d_wv), (1, d_wk)):
        for i in range(groups):
            value = weights[which * groups + i].reshape(D_LAT, PAIR * 128)
            out[:, i * PAIR * 128:(i + 1) * PAIR * 128] = value.astype(F32)


def local(n_ctx, n_head, latent, q_nope, q_rope, grad_out, w_uk, w_uv, stretch_order):
    heads = w_uk.shape[1] // D_NOPE
    groups = heads // PAIR
    pieces = 2 * groups
    rows = heads * TOK
    n_keys = n_ctx * TOK
    own = TOK // n_head
    part = (D_LAT // (2 * n_ctx), PAIR * 128)
    vmem = pl.BlockSpec(memory_space=pltpu.VMEM)
    dma = pltpu.SemaphoreType.DMA
    lat_out, qn_out, qr_out, weights = pl.pallas_call(
        functools.partial(body, n_ctx, n_head, groups),
        out_shape=(
            jax.ShapeDtypeStruct((own, WIDTH), F32),
            jax.ShapeDtypeStruct(q_nope.shape, BF16),
            jax.ShapeDtypeStruct(q_rope.shape, BF16),
            jax.ShapeDtypeStruct((pieces, 2, n_ctx) + part, BF16),
        ),
        in_specs=[vmem] * 6 + [pl.BlockSpec(memory_space=pltpu.SMEM)],
        out_specs=(vmem,) * 4,
        scratch_shapes=[
            pltpu.VMEM((2, WIDTH // 2, n_keys), BF16),
            pltpu.VMEM((rows, WIDTH), BF16),
            pltpu.VMEM((rows, D_LAT), BF16),
            pltpu.VMEM((rows, WIDTH), BF16),
            pltpu.VMEM((1, n_keys), jnp.int32),
            pltpu.VMEM((PAIR * TOK, 1), jnp.int32),
            pltpu.VMEM((rows, n_keys), BF16),
            pltpu.VMEM((rows, n_keys), BF16),
            pltpu.VMEM((pieces, 2, n_ctx) + part, BF16),
            pltpu.VMEM((pieces, n_ctx) + part, BF16),
            pltpu.VMEM((pieces, n_ctx) + part, BF16),
            pltpu.VMEM((pieces, n_ctx) + part, BF16),
            pltpu.VMEM((pieces, n_ctx) + part, BF16),
            pltpu.VMEM((pieces,) + part, BF16),
            pltpu.VMEM((n_head, n_ctx, own, WIDTH), BF16),
            pltpu.VMEM((n_head, n_ctx, own, WIDTH), BF16),
            pltpu.VMEM((n_ctx - 1, own, WIDTH), BF16),
            pltpu.VMEM((n_ctx - 1, own, WIDTH), BF16),
            dma((n_ctx - 1,)), dma((n_ctx - 1,)),
            dma((n_ctx - 1,)), dma((n_ctx - 1,)),
            dma((pieces,)), dma((pieces,)),
            dma((pieces, n_ctx - 1)), dma((pieces, n_ctx - 1)),
            dma((pieces, n_ctx - 1)), dma((pieces, n_ctx - 1)),
            dma((pieces, n_ctx)), dma((pieces, n_ctx)),
            dma((n_head - 1,)), dma((n_head - 1,)),
            dma((n_ctx - 1,)), dma((n_ctx - 1,)),
            dma((pieces,)), dma((pieces,)), dma((pieces,)), dma((1,)),
        ],
        compiler_params=pltpu.CompilerParams(
            collective_id=0, has_side_effects=True, vmem_limit_bytes=56 << 20
        ),
    )(latent.transpose(0, 2, 1).reshape(2, WIDTH // 2, TOK), q_nope, q_rope, grad_out, w_uk, w_uv,
      stretch_order)
    return pl.pallas_call(
        functools.partial(finish, groups),
        out_shape=(
            jax.ShapeDtypeStruct((1, own, WIDTH), F32),
            jax.ShapeDtypeStruct(q_nope.shape, BF16),
            jax.ShapeDtypeStruct(q_rope.shape, BF16),
            jax.ShapeDtypeStruct(w_uk.shape, F32),
            jax.ShapeDtypeStruct(w_uv.shape, F32),
        ),
        in_specs=[vmem] * 4,
        out_specs=(vmem,) * 5,
        compiler_params=pltpu.CompilerParams(vmem_limit_bytes=16 << 20),
    )(lat_out, qn_out, qr_out, weights)


def solution(mesh):
    n_ctx, n_head = mesh.shape["ctx"], mesh.shape["head"]
    placed = (
        P("dp", "ctx", None),
        P("dp", "ctx", "head"),
        P("dp", "ctx", "head"),
        P("dp", "ctx", "head"),
        P(None, "head"),
        P(None, "head"),
        P(),
    )
    return jax.shard_map(
        functools.partial(local, n_ctx, n_head),
        mesh=mesh,
        in_specs=placed,
        out_specs=(
            P("dp", ("ctx", "head"), None),
            P("dp", "ctx", "head"),
            P("dp", "ctx", "head"),
            P(None, "head"),
            P(None, "head"),
        ),
        check_vma=False,
    )
```

time: 70.6 us -> 60.8 us (0.86)
  Pallas kernels: 61.6 us -> 56.1 us
  local copies, waits for them, and re-layouts: 8.1 us -> 3.85 us
    pallas_call x1 -> x2, Pallas kernels: 61.6 us -> 56.1 us  [the longest x1 54.6 us: local(): pl.pallas_call(functools.partial(body, n_ctx, n_head, groups), out_shape=...]
    unnamed x12 -> x8, local copies, waits for them, and re-layouts: 8.1 us -> 3.85 us
where the time goes in v2:
time: 60.8 us; the launch traced here: 60.6 us
  Pallas kernels  56.1 us (92%)
  local copies, waits for them, and re-layouts  3.85 us (6%)
  between operations  0.65 us (1%)
    pallas_call x1, Pallas kernels, local(): pl.pallas_call(functools.partial(body, n_ctx, n_head, groups), out_shape=...  54.6 us
    unnamed x8, local copies, waits for them, and re-layouts  3.85 us
    pallas_call x1, Pallas kernels, local(): pl.pallas_call(functools.partial(finish, groups), out_shape=(jax.ShapeDty...  1.49 us

profile of v2, /device:TPU:0, one launch (start us, length us, event | category | flops | bytes accessed | tf_op | source)
XLA Modules:
  0.0 60.6 jit_solution(16245819810628502856)
XLA Ops:
  0.6 54.6 %shard_map.110 = (f32[32,576]{1,0:T(8,128)}, bf16[1,128,512]{2,1,0:T(8,128)(2,1)}, bf16[1,128,256]{2,1,0:T(8,128)(2,1)}, bf16[4,2,4,64,256]{4,3,2,1,0:T(8,128)(2,1)}) custom-call(bf16[2,288,128]{2,1,0:T(8,128)(2,1)} %bitcast.3, bf16[1,128,512]{2,1,0:T(8,128)(2,1)} %qn.1, bf16[1,128,256]{2,1,0:T(8,128)(2,1)} %qr.1, bf16[1,128,512]{2,1,0:T(8,128)(2,1)} %g.1, ...), custom_call_target="tpu_custom_call" | custom-call | tf_op jit(solution)/shard_map/pallas_call | solution.py:321
  55.2 0.0 copy-start
  55.2 1.2 %copy-done = bf16[4,2,4,64,256]{4,3,2,1,0:T(8,128)(2,1)S(1)} copy-done((bf16[4,2,4,64,256]{4,3,2,1,0:T(8,128)(2,1)S(1)}, bf16[4,2,4,64,256]{4,3,2,1,0:T(8,128)(2,1)}, u32[]{:S(2)}) %copy-start) | copy-done | bytes 1048600
  56.4 0.0 copy-start.1
  56.4 0.9 %copy-done.1 = bf16[1,128,512]{2,1,0:T(8,128)(2,1)S(1)} copy-done((bf16[1,128,512]{2,1,0:T(8,128)(2,1)S(1)}, bf16[1,128,512]{2,1,0:T(8,128)(2,1)}, u32[]{:S(2)}) %copy-start.1) | copy-done | bytes 131096
  57.3 0.0 copy-start.2
  57.3 0.9 %copy-done.2 = f32[32,576]{1,0:T(8,128)S(1)} copy-done((f32[32,576]{1,0:T(8,128)S(1)}, f32[32,576]{1,0:T(8,128)}, u32[]{:S(2)}) %copy-start.2) | copy-done | bytes 73752
  58.2 0.0 copy-start.3
  58.2 0.8 %copy-done.3 = bf16[1,128,256]{2,1,0:T(8,128)(2,1)S(1)} copy-done((bf16[1,128,256]{2,1,0:T(8,128)(2,1)S(1)}, bf16[1,128,256]{2,1,0:T(8,128)(2,1)}, u32[]{:S(2)}) %copy-start.3) | copy-done | bytes 65560
  59.1 1.5 %shard_map.111 = (f32[1,32,576]{2,1,0:T(8,128)}, bf16[1,128,512]{2,1,0:T(8,128)(2,1)}, bf16[1,128,256]{2,1,0:T(8,128)(2,1)}, f32[512,512]{1,0:T(8,128)}, f32[512,512]{1,0:T(8,128)}) custom-call(f32[32,576]{1,0:T(8,128)S(1)} %copy-done.2, bf16[1,128,512]{2,1,0:T(8,128)(2,1)S(1)} %copy-done.1, bf16[1,128,256]{2,1,0:T(8,128)(2,1)S(1)} %copy-done.3, ...), custom_call_target="tpu_custom_call" | custom-call | tf_op jit(solution)/shard_map/pallas_call | solution.py:365
Async XLA Ops:
  55.2 1.2 %copy-start = (bf16[4,2,4,64,256]{4,3,2,1,0:T(8,128)(2,1)S(1)}, bf16[4,2,4,64,256]{4,3,2,1,0:T(8,128)(2,1)}, u32[]{:S(2)}) copy-start(bf16[4,2,4,64,256]{4,3,2,1,0:T(8,128)(2,1)} %get-tuple-element.12.weights) | copy-start | bytes 3145732
  56.4 0.9 %copy-start.1 = (bf16[1,128,512]{2,1,0:T(8,128)(2,1)S(1)}, bf16[1,128,512]{2,1,0:T(8,128)(2,1)}, u32[]{:S(2)}) copy-start(bf16[1,128,512]{2,1,0:T(8,128)(2,1)} %get-tuple-element.10.qn) | copy-start | bytes 393220
  57.3 0.9 %copy-start.2 = (f32[32,576]{1,0:T(8,128)S(1)}, f32[32,576]{1,0:T(8,128)}, u32[]{:S(2)}) copy-start(f32[32,576]{1,0:T(8,128)} %get-tuple-element.9.lat) | copy-start | bytes 221188
  58.2 0.8 %copy-start.3 = (bf16[1,128,256]{2,1,0:T(8,128)(2,1)S(1)}, bf16[1,128,256]{2,1,0:T(8,128)(2,1)}, u32[]{:S(2)}) copy-start(bf16[1,128,256]{2,1,0:T(8,128)(2,1)} %get-tuple-element.11.qr) | copy-start | bytes 196612

commit v3 on v2

--- a/solution.py
+++ b/solution.py
@@ -14,7 +14,7 @@
 D_V = 128
 TOK = 128
 STRETCH = 64
-PAIR = 2
+PAIR = 1
 WIDTH = D_LAT + D_ROPE
 SCALE = 1.0 / math.sqrt(D_NOPE + D_ROPE)
 MESH = pl.DeviceIdType.MESH
@@ -36,12 +36,13 @@
 
 def body(
     n_ctx, n_head, groups,
-    lat, qn, qr, g, wk, wv, order,
+    lat, qn_in, qr_in, g_in, wk_in, wv_in, order,
     d_lat, d_qn, d_qr, final,
+    qn, qr, g, wk, wv,
     gath, qc, gl, ql, key_pos, row_pos, pb, ds,
     wpart, yown, yrecv, zsend, zrecv, own, gsend, hrecv, lsend, lrecv,
     lat_s, lat_r, fwd_s, fwd_r, y_s, y_r, z_s, z_r, ag_s, ag_r, yag_s, yag_r, h_s, h_r, l_s, l_r,
-    yown_s, zown_s, own_s, hown_s,
+    yown_s, zown_s, own_s, hown_s, in_s,
 ):
     rep = lax.axis_index("dp")
     ctx = lax.axis_index("ctx")
@@ -118,6 +119,15 @@
         return copy(lsend.at[k - 1], lrecv.at[k - 1], l_s.at[k - 1], l_r.at[k - 1],
                     (rep, ctx_at(-k), head))
 
+    fetches = [
+        pltpu.make_async_copy(src, dst, in_s.at[i])
+        for i, (src, dst) in enumerate((
+            (lat, gath.at[:, :, :TOK]), (qn_in, qn), (wk_in, wk), (g_in, g), (wv_in, wv), (qr_in, qr),
+        ))
+    ]
+    for c in fetches:
+        c.start()
+
     partners = [(rep, ctx_at(k), head) for k in ctx_steps]
     partners += [(rep, ctx, head_at(k)) for k in range(1, n_head)]
     partners += [(other, ctx, head)]
@@ -128,7 +138,8 @@
 
     for k in ctx_steps:
         lat_copy(k).start()
-    gath[:, :, :TOK] = lat[...]
+    for c in fetches:
+        c.wait()
 
     def project(i):
         for sub in range(PAIR):
@@ -167,7 +178,21 @@
         y_keep(p).start()
         y_copy(p).start()
 
+    def spread(p):
+        y_keep(p).wait()
+        y_copy(p).wait_recv()
+
+        def add(i):
+            total = yown[p, i].astype(F32) + yrecv[p, i].astype(F32)
+            zsend[p, i] = total.astype(BF16)
+
+        each(0, n_ctx, add)
+        z_keep(p).start()
+        for k in ctx_steps:
+            z_copy(p, k).start()
+
     def attend(i):
+        pl.when(i >= 2)(lambda: spread(i - 2))
         rows = tile(i, PAIR * TOK)
         keys = gath[...].reshape(WIDTH, n_keys)
         score = dot_nn(qc[rows, :], keys) * SCALE
@@ -182,21 +207,8 @@
         out_low = dot_nt(low, keys[:D_LAT, :]).astype(BF16)
         weight_term(i, out_low, g, i)
 
-    def spread(p):
-        y_keep(p).wait()
-        y_copy(p).wait_recv()
-
-        def add(i):
-            total = yown[p, i].astype(F32) + yrecv[p, i].astype(F32)
-            zsend[p, i] = total.astype(BF16)
-
-        each(0, n_ctx, add)
-        z_keep(p).start()
-        for k in ctx_steps:
-            z_copy(p, k).start()
-
     def query_side(i):
-        spread(i)
+        spread(groups + i - 2)
         rows = tile(i, PAIR * TOK)
         keys = gath[...].reshape(WIDTH, n_keys)
         low = dot_nt(ds[rows, :], keys).astype(BF16)
@@ -215,9 +227,9 @@
 
     each(0, groups, attend)
     each(0, groups, query_side)
-    for i in range(groups):
-        each(i * n_ctx // groups, (i + 1) * n_ctx // groups, key_side)
-        spread(groups + i)
+    for i in range(2):
+        each(i * n_ctx // 2, (i + 1) * n_ctx // 2, key_side)
+        spread(pieces - 2 + i)
     h_keep = pltpu.make_async_copy(gsend.at[head], hrecv.at[n_head - 1], hown_s.at[0])
     h_keep.start()
     for k in range(1, n_head):
@@ -265,14 +277,14 @@
                 lsend[k - 1] = total.astype(BF16)
                 l_copy(k).start()
 
-    for p in range(groups):
+    def settle_next(p):
         settle(p)
+        hand_on(p - groups)
+
+    each(0, groups, settle)
     latent_terms()
-    for p in range(groups):
-        settle(groups + p)
-        hand_on(p)
-    for p in range(groups):
-        hand_on(groups + p)
+    each(groups, pieces, settle_next)
+    each(groups, pieces, hand_on)
     total = d_lat[...]
     for k in ctx_steps:
         l_copy(k).wait_recv()
@@ -285,7 +297,8 @@
         l_copy(k).wait_send()
     for k in range(1, n_head):
         h_copy(k).wait_send()
-    for p in range(pieces):
+
+    def end(p):
         y_copy(p).wait_send()
         own_keep(p).wait()
         for k in ctx_steps:
@@ -297,15 +310,22 @@
             arrived.wait_recv()
             yag_copy(p, k).wait_send()
 
-
-def finish(groups, lat, qn, qr, weights, d_lat, d_qn, d_qr, d_wk, d_wv):
-    d_lat[0] = lat[...]
-    d_qn[...] = qn[...]
-    d_qr[...] = qr[...]
+    each(0, pieces, end)
+
+
+def finish(groups, lat, qn, qr, weights, d_lat, d_qn, d_qr, d_wk, d_wv, sems):
+    moves = [
+        pltpu.make_async_copy(src, dst, sems.at[i])
+        for i, (src, dst) in enumerate(((lat, d_lat.at[0]), (qn, d_qn), (qr, d_qr)))
+    ]
+    for c in moves:
+        c.start()
     for which, out in ((0, d_wv), (1, d_wk)):
         for i in range(groups):
             value = weights[which * groups + i].reshape(D_LAT, PAIR * 128)
             out[:, i * PAIR * 128:(i + 1) * PAIR * 128] = value.astype(F32)
+    for c in moves:
+        c.wait()
 
 
 def local(n_ctx, n_head, latent, q_nope, q_rope, grad_out, w_uk, w_uv, stretch_order):
@@ -317,6 +337,7 @@
     own = TOK // n_head
     part = (D_LAT // (2 * n_ctx), PAIR * 128)
     vmem = pl.BlockSpec(memory_space=pltpu.VMEM)
+    anywhere = pl.BlockSpec(memory_space=pl.ANY)
     dma = pltpu.SemaphoreType.DMA
     lat_out, qn_out, qr_out, weights = pl.pallas_call(
         functools.partial(body, n_ctx, n_head, groups),
@@ -326,9 +347,14 @@
             jax.ShapeDtypeStruct(q_rope.shape, BF16),
             jax.ShapeDtypeStruct((pieces, 2, n_ctx) + part, BF16),
         ),
-        in_specs=[vmem] * 6 + [pl.BlockSpec(memory_space=pltpu.SMEM)],
+        in_specs=[anywhere] * 6 + [pl.BlockSpec(memory_space=pltpu.SMEM)],
         out_specs=(vmem,) * 4,
         scratch_shapes=[
+            pltpu.VMEM(q_nope.shape, BF16),
+            pltpu.VMEM(q_rope.shape, BF16),
+            pltpu.VMEM(grad_out.shape, BF16),
+            pltpu.VMEM(w_uk.shape, BF16),
+            pltpu.VMEM(w_uv.shape, BF16),
             pltpu.VMEM((2, WIDTH // 2, n_keys), BF16),
             pltpu.VMEM((rows, WIDTH), BF16),
             pltpu.VMEM((rows, D_LAT), BF16),
@@ -355,7 +381,7 @@
             dma((pieces, n_ctx)), dma((pieces, n_ctx)),
             dma((n_head - 1,)), dma((n_head - 1,)),
             dma((n_ctx - 1,)), dma((n_ctx - 1,)),
-            dma((pieces,)), dma((pieces,)), dma((pieces,)), dma((1,)),
+            dma((pieces,)), dma((pieces,)), dma((pieces,)), dma((1,)), dma((6,)),
         ],
         compiler_params=pltpu.CompilerParams(
             collective_id=0, has_side_effects=True, vmem_limit_bytes=56 << 20
@@ -371,9 +397,10 @@
             jax.ShapeDtypeStruct(w_uk.shape, F32),
             jax.ShapeDtypeStruct(w_uv.shape, F32),
         ),
-        in_specs=[vmem] * 4,
-        out_specs=(vmem,) * 5,
-        compiler_params=pltpu.CompilerParams(vmem_limit_bytes=16 << 20),
+        in_specs=[anywhere] * 3 + [vmem],
+        out_specs=(anywhere,) * 3 + (vmem,) * 2,
+        scratch_shapes=[dma((3,))],
+        compiler_params=pltpu.CompilerParams(vmem_limit_bytes=60 << 20),
     )(lat_out, qn_out, qr_out, weights)
 
 

time: 60.8 us -> 70.4 us (1.16)
  Pallas kernels: 56.1 us -> 69.6 us
  local copies, waits for them, and re-layouts: 3.85 us -> 0 us
    pallas_call x1, Pallas kernels: 1.49 us -> 12.1 us  [local(): pl.pallas_call(functools.partial(finish, groups), out_shape=(jax.ShapeDty...]
    unnamed x8 -> x0, local copies, waits for them, and re-layouts: 3.85 us -> none
    pallas_call x1, Pallas kernels: 54.6 us -> 57.5 us  [local(): pl.pallas_call(functools.partial(body, n_ctx, n_head, groups), out_shape=...]
where the time goes in v3:
time: 70.4 us; the launch traced here: 70.2 us
  Pallas kernels  69.6 us (99%)
    pallas_call x1, Pallas kernels, local(): pl.pallas_call(functools.partial(body, n_ctx, n_head, groups), out_shape=...  57.5 us
    pallas_call x1, Pallas kernels, local(): pl.pallas_call(functools.partial(finish, groups), out_shape=(jax.ShapeDty...  12.1 us

profile of v3, /device:TPU:0, one launch (start us, length us, event | category | flops | bytes accessed | tf_op | source)
XLA Modules:
  0.0 70.2 jit_solution(1728639697743628459)
XLA Ops:
  0.6 57.5 %shard_map.110 = (f32[32,576]{1,0:T(8,128)}, bf16[1,128,512]{2,1,0:T(8,128)(2,1)}, bf16[1,128,256]{2,1,0:T(8,128)(2,1)}, bf16[8,2,4,64,128]{4,3,2,1,0:T(8,128)(2,1)}) custom-call(bf16[2,288,128]{2,1,0:T(8,128)(2,1)} %bitcast.3, bf16[1,128,512]{2,1,0:T(8,128)(2,1)} %qn_in.1, bf16[1,128,256]{2,1,0:T(8,128)(2,1)} %qr_in.1, bf16[1,128,512]{2,1,0:T(8,128)(2,1)} %g_in.1, ...), custom_call_target="tpu_custom_call" | custom-call | tf_op jit(solution)/shard_map/pallas_call | solution.py:342
  58.1 12.1 %shard_map.111 = (f32[1,32,576]{2,1,0:T(8,128)}, bf16[1,128,512]{2,1,0:T(8,128)(2,1)}, bf16[1,128,256]{2,1,0:T(8,128)(2,1)}, f32[512,512]{1,0:T(8,128)}, f32[512,512]{1,0:T(8,128)}) custom-call(f32[32,576]{1,0:T(8,128)} %get-tuple-element.9.lat, bf16[1,128,512]{2,1,0:T(8,128)(2,1)} %get-tuple-element.10.qn, bf16[1,128,256]{2,1,0:T(8,128)(2,1)} %get-tuple-element.11.qr, ...), custom_call_target="tpu_custom_call" | custom-call | tf_op jit(solution)/shard_map/pallas_call | solution.py:391

commit v4 on v3

--- a/solution.py
+++ b/solution.py
@@ -14,7 +14,7 @@
 D_V = 128
 TOK = 128
 STRETCH = 64
-PAIR = 1
+PAIR = 2
 WIDTH = D_LAT + D_ROPE
 SCALE = 1.0 / math.sqrt(D_NOPE + D_ROPE)
 MESH = pl.DeviceIdType.MESH
@@ -39,7 +39,7 @@
     lat, qn_in, qr_in, g_in, wk_in, wv_in, order,
     d_lat, d_qn, d_qr, final,
     qn, qr, g, wk, wv,
-    gath, qc, gl, ql, key_pos, row_pos, pb, ds,
+    gath, keys_n, qc, gl, qct, glt, qlt, bias, pbt, dst,
     wpart, yown, yrecv, zsend, zrecv, own, gsend, hrecv, lsend, lrecv,
     lat_s, lat_r, fwd_s, fwd_r, y_s, y_r, z_s, z_r, ag_s, ag_r, yag_s, yag_r, h_s, h_r, l_s, l_r,
     yown_s, zown_s, own_s, hown_s, in_s,
@@ -144,36 +144,46 @@
     def project(i):
         for sub in range(PAIR):
             rows = tile(i * PAIR + sub, 128)
-            qc[rows, :D_LAT] = dot_nt(qn[0, :, rows], wk[:, rows]).astype(BF16)
-            gl[rows, :] = dot_nt(g[0, :, rows], wv[:, rows]).astype(BF16)
+            qn_h, g_h, wk_h, wv_h = qn[0, :, rows], g[0, :, rows], wk[:, rows], wv[:, rows]
+            qc[rows, :D_LAT] = dot_nt(qn_h, wk_h).astype(BF16)
+            gl[rows, :] = dot_nt(g_h, wv_h).astype(BF16)
+            qct[:D_LAT, rows] = dot_nt(wk_h, qn_h).astype(BF16)
+            glt[:, rows] = dot_nt(wv_h, g_h).astype(BF16)
 
     each(0, groups, project)
+    rope_t = qr[0].T
     for m in range(groups * PAIR):
-        qc[m * TOK:(m + 1) * TOK, D_LAT:] = qr[0, :, m * D_ROPE:(m + 1) * D_ROPE]
-
-    lane = lax.broadcasted_iota(jnp.int32, (1, n_keys), 1)
-    start_pos = jnp.zeros((1, n_keys), jnp.int32)
+        rows, cols = slice(m * TOK, (m + 1) * TOK), slice(m * D_ROPE, (m + 1) * D_ROPE)
+        qc[rows, D_LAT:] = qr[0, :, cols]
+        qct[D_LAT:, rows] = rope_t[cols, :]
+
+    lane = lax.broadcasted_iota(jnp.int32, (1, PAIR * TOK), 1) % TOK
+    row_start = jnp.where(lane < STRETCH, order[2 * ctx], order[2 * ctx + 1]) * STRETCH
+    row_pos = row_start + lane % STRETCH
+    inner = lax.broadcasted_iota(jnp.int32, (STRETCH, PAIR * TOK), 0)
     for k in range(n_ctx):
         owner = ctx_at(-k)
         for part in range(2):
+            key_pos = inner + order[2 * owner + part] * STRETCH
             first = k * TOK + part * STRETCH
-            inside = (lane >= first) & (lane < first + STRETCH)
-            start_pos = start_pos + jnp.where(inside, order[2 * owner + part] * STRETCH, 0)
-    key_pos[...] = start_pos + lane % STRETCH
-    row = lax.broadcasted_iota(jnp.int32, (PAIR * TOK, 1), 0) % TOK
-    row_start = jnp.where(row < STRETCH, order[2 * ctx], order[2 * ctx + 1]) * STRETCH
-    row_pos[...] = row_start + row % STRETCH
-
+            bias[first:first + STRETCH, :] = jnp.where(key_pos <= row_pos, 0.0, -jnp.inf)
+
+    def turn(k):
+        rows = slice(k * TOK, (k + 1) * TOK)
+        keys_n[rows, :] = gath[:, :, rows].reshape(WIDTH, TOK).T
+
+    turn(0)
     for k in ctx_steps:
         lat_copy(k).wait_recv()
         fwd_copy(k).start()
     for k in ctx_steps:
         fwd_copy(k).wait_recv()
+        turn(k)
 
     def weight_term(p, low, value, i):
         for sub in range(PAIR):
             cols = tile(i * PAIR + sub, 128)
-            term = dot_tn(low[sub * TOK:(sub + 1) * TOK, :D_LAT], value[0, :, cols]).astype(BF16)
+            term = dot_nn(low[:D_LAT, sub * TOK:(sub + 1) * TOK], value[0, :, cols]).astype(BF16)
             wpart[p, :, :, :, sub * 128:(sub + 1) * 128] = term.reshape(2, n_ctx, part_rows, 128)
         y_keep(p).start()
         y_copy(p).start()
@@ -192,35 +202,34 @@
             z_copy(p, k).start()
 
     def attend(i):
-        pl.when(i >= 2)(lambda: spread(i - 2))
+        if groups > 2:
+            pl.when(i >= 2)(lambda: spread(i - 2))
         rows = tile(i, PAIR * TOK)
+        score = dot_nn(keys_n[...], qct[:, rows]) * SCALE + bias[...]
+        expo = jnp.exp(score - jnp.max(score, axis=0, keepdims=True))
+        prob = expo * (1.0 / jnp.sum(expo, axis=0, keepdims=True))
+        low = prob.astype(BF16)
+        pbt[:, rows] = low
+        grad = dot_nn(keys_n[:, :D_LAT], glt[:, rows])
+        delta = jnp.sum(prob * grad, axis=0, keepdims=True)
+        dst[:, rows] = (SCALE * prob * (grad - delta)).astype(BF16)
         keys = gath[...].reshape(WIDTH, n_keys)
-        score = dot_nn(qc[rows, :], keys) * SCALE
-        score = jnp.where(key_pos[...] <= row_pos[...], score, -jnp.inf)
-        expo = jnp.exp(score - jnp.max(score, axis=1, keepdims=True))
-        prob = expo * (1.0 / jnp.sum(expo, axis=1, keepdims=True))
-        low = prob.astype(BF16)
-        pb[rows, :] = low
-        grad = dot_nn(gl[rows, :], keys[:D_LAT, :])
-        delta = jnp.sum(prob * grad, axis=1, keepdims=True)
-        ds[rows, :] = (SCALE * prob * (grad - delta)).astype(BF16)
-        out_low = dot_nt(low, keys[:D_LAT, :]).astype(BF16)
-        weight_term(i, out_low, g, i)
+        weight_term(i, dot_nn(keys[:D_LAT, :], low).astype(BF16), g, i)
 
     def query_side(i):
         spread(groups + i - 2)
         rows = tile(i, PAIR * TOK)
         keys = gath[...].reshape(WIDTH, n_keys)
-        low = dot_nt(ds[rows, :], keys).astype(BF16)
-        ql[rows, :] = low
+        low = dot_nn(keys, dst[:, rows]).astype(BF16)
+        qlt[:, rows] = low
         weight_term(groups + i, low, qn, i)
 
     own_rows = TOK // n_head
 
     def key_side(k):
         cols = tile(k, TOK)
-        value = dot_tn(pb[:, cols], gl[...])
-        key = dot_tn(ds[:, cols], qc[...])
+        value = dot_nn(pbt[cols, :], gl[...])
+        key = dot_nn(dst[cols, :], qc[...])
         low = key[:, :D_LAT] + value
         gsend[:, k, :, :D_LAT] = low.reshape(n_head, own_rows, D_LAT).astype(BF16)
         gsend[:, k, :, D_LAT:] = key[:, D_LAT:].reshape(n_head, own_rows, D_ROPE).astype(BF16)
@@ -238,11 +247,11 @@
     def nope(i):
         for sub in range(PAIR):
             rows = tile(i * PAIR + sub, 128)
-            d_qn[0, :, rows] = dot_nn(ql[rows, :D_LAT], wk[:, rows]).astype(BF16)
+            d_qn[0, :, rows] = dot_tn(qlt[:D_LAT, rows], wk[:, rows]).astype(BF16)
 
     each(0, groups, nope)
     for m in range(groups * PAIR):
-        d_qr[0, :, m * D_ROPE:(m + 1) * D_ROPE] = ql[m * TOK:(m + 1) * TOK, D_LAT:]
+        d_qr[0, :, m * D_ROPE:(m + 1) * D_ROPE] = qlt[D_LAT:, m * TOK:(m + 1) * TOK].T
 
     def settle(p):
         z_keep(p).wait()
@@ -313,19 +322,14 @@
     each(0, pieces, end)
 
 
-def finish(groups, lat, qn, qr, weights, d_lat, d_qn, d_qr, d_wk, d_wv, sems):
-    moves = [
-        pltpu.make_async_copy(src, dst, sems.at[i])
-        for i, (src, dst) in enumerate(((lat, d_lat.at[0]), (qn, d_qn), (qr, d_qr)))
-    ]
-    for c in moves:
-        c.start()
+def finish(groups, lat, qn, qr, weights, d_lat, d_qn, d_qr, d_wk, d_wv):
+    d_lat[0] = lat[...]
+    d_qn[...] = qn[...]
+    d_qr[...] = qr[...]
     for which, out in ((0, d_wv), (1, d_wk)):
         for i in range(groups):
             value = weights[which * groups + i].reshape(D_LAT, PAIR * 128)
             out[:, i * PAIR * 128:(i + 1) * PAIR * 128] = value.astype(F32)
-    for c in moves:
-        c.wait()
 
 
 def local(n_ctx, n_head, latent, q_nope, q_rope, grad_out, w_uk, w_uv, stretch_order):
@@ -356,13 +360,15 @@
             pltpu.VMEM(w_uk.shape, BF16),
             pltpu.VMEM(w_uv.shape, BF16),
             pltpu.VMEM((2, WIDTH // 2, n_keys), BF16),
+            pltpu.VMEM((n_keys, WIDTH), BF16),
             pltpu.VMEM((rows, WIDTH), BF16),
             pltpu.VMEM((rows, D_LAT), BF16),
-            pltpu.VMEM((rows, WIDTH), BF16),
-            pltpu.VMEM((1, n_keys), jnp.int32),
-            pltpu.VMEM((PAIR * TOK, 1), jnp.int32),
-            pltpu.VMEM((rows, n_keys), BF16),
-            pltpu.VMEM((rows, n_keys), BF16),
+            pltpu.VMEM((WIDTH, rows), BF16),
+            pltpu.VMEM((D_LAT, rows), BF16),
+            pltpu.VMEM((WIDTH, rows), BF16),
+            pltpu.VMEM((n_keys, PAIR * TOK), F32),
+            pltpu.VMEM((n_keys, rows), BF16),
+            pltpu.VMEM((n_keys, rows), BF16),
             pltpu.VMEM((pieces, 2, n_ctx) + part, BF16),
             pltpu.VMEM((pieces, n_ctx) + part, BF16),
             pltpu.VMEM((pieces, n_ctx) + part, BF16),
@@ -397,9 +403,8 @@
             jax.ShapeDtypeStruct(w_uk.shape, F32),
             jax.ShapeDtypeStruct(w_uv.shape, F32),
         ),
-        in_specs=[anywhere] * 3 + [vmem],
-        out_specs=(anywhere,) * 3 + (vmem,) * 2,
-        scratch_shapes=[dma((3,))],
+        in_specs=[vmem] * 4,
+        out_specs=(vmem,) * 5,
         compiler_params=pltpu.CompilerParams(vmem_limit_bytes=60 << 20),
     )(lat_out, qn_out, qr_out, weights)
 

time: 70.4 us -> 58 us (0.82)
  Pallas kernels: 69.6 us -> 57.2 us
    pallas_call x1, Pallas kernels: 12.1 us -> 2.81 us  [local(): pl.pallas_call(functools.partial(finish, groups), out_shape=(jax.ShapeDty...]
    pallas_call x1, Pallas kernels: 57.5 us -> 54.3 us  [local(): pl.pallas_call(functools.partial(body, n_ctx, n_head, groups), out_shape=...]
where the time goes in v4:
time: 58 us; the launch traced here: 57.8 us
  Pallas kernels  57.2 us (99%)
  between operations  0.64 us (1%)
    pallas_call x1, Pallas kernels, local(): pl.pallas_call(functools.partial(body, n_ctx, n_head, groups), out_shape=...  54.3 us
    pallas_call x1, Pallas kernels, local(): pl.pallas_call(functools.partial(finish, groups), out_shape=(jax.ShapeDty...  2.81 us

profile of v4, /device:TPU:0, one launch (start us, length us, event | category | flops | bytes accessed | tf_op | source)
XLA Modules:
  0.0 57.8 jit_solution(3093387776452099981)
XLA Ops:
  0.6 54.3 %shard_map.110 = (f32[32,576]{1,0:T(8,128)}, bf16[1,128,512]{2,1,0:T(8,128)(2,1)}, bf16[1,128,256]{2,1,0:T(8,128)(2,1)}, bf16[4,2,4,64,256]{4,3,2,1,0:T(8,128)(2,1)}) custom-call(bf16[2,288,128]{2,1,0:T(8,128)(2,1)} %bitcast.3, bf16[1,128,512]{2,1,0:T(8,128)(2,1)} %qn_in.1, bf16[1,128,256]{2,1,0:T(8,128)(2,1)} %qr_in.1, bf16[1,128,512]{2,1,0:T(8,128)(2,1)} %g_in.1, ...), custom_call_target="tpu_custom_call" | custom-call | tf_op jit(solution)/shard_map/pallas_call | solution.py:346
  55.0 2.8 %shard_map.111 = (f32[1,32,576]{2,1,0:T(8,128)}, bf16[1,128,512]{2,1,0:T(8,128)(2,1)}, bf16[1,128,256]{2,1,0:T(8,128)(2,1)}, f32[512,512]{1,0:T(8,128)}, f32[512,512]{1,0:T(8,128)}) custom-call(f32[32,576]{1,0:T(8,128)} %get-tuple-element.9.lat, bf16[1,128,512]{2,1,0:T(8,128)(2,1)} %get-tuple-element.10.qn, bf16[1,128,256]{2,1,0:T(8,128)(2,1)} %get-tuple-element.11.qr, ...), custom_call_target="tpu_custom_call" | custom-call | tf_op jit(solution)/shard_map/pallas_call | solution.py:397

commit v5 on v4

--- a/solution.py
+++ b/solution.py
@@ -40,9 +40,9 @@
     d_lat, d_qn, d_qr, final,
     qn, qr, g, wk, wv,
     gath, keys_n, qc, gl, qct, glt, qlt, bias, pbt, dst,
-    wpart, yown, yrecv, zsend, zrecv, own, gsend, hrecv, lsend, lrecv,
+    wpart, yown, yrecv, gsend, hrecv, lsend, lrecv,
     lat_s, lat_r, fwd_s, fwd_r, y_s, y_r, z_s, z_r, ag_s, ag_r, yag_s, yag_r, h_s, h_r, l_s, l_r,
-    yown_s, zown_s, own_s, hown_s, in_s,
+    yown_s, hown_s, in_s, *held,
 ):
     rep = lax.axis_index("dp")
     ctx = lax.axis_index("ctx")
@@ -51,7 +51,13 @@
     half = lax.rem(head, 2)
     sibling = head + 1 - 2 * half
     pieces = 2 * groups
-    part_rows = own.shape[1]
+    part_rows = wpart.shape[3]
+    levels = n_ctx.bit_length() - 1
+    held, got = held[:levels], held[levels:]
+    bits = [lax.rem(ctx // (1 << v), 2) for v in range(levels)]
+    mates = [(rep, ctx + (1 - 2 * bits[v]) * (1 << v), head) for v in range(levels)]
+    spans = [n_ctx >> (v + 1) for v in range(levels)]
+    begins = [sum(bits[u] * spans[u] for u in range(v + 1)) for v in range(levels)]
     n_keys = n_ctx * TOK
     ctx_steps = range(1, n_ctx)
 
@@ -92,24 +98,24 @@
     def y_keep(p):
         return pltpu.make_async_copy(wpart.at[p, rep], yown.at[p], yown_s.at[p])
 
-    def z_copy(p, k):
-        return copy(zsend.at[p, ctx_at(k)], zrecv.at[p, k - 1], z_s.at[p, k - 1], z_r.at[p, k - 1],
-                    (rep, ctx_at(k), head))
-
-    def z_keep(p):
-        return pltpu.make_async_copy(zsend.at[p, ctx], zrecv.at[p, n_ctx - 1], zown_s.at[p])
-
-    def ag_copy(p, k):
-        return copy(own.at[p], final.at[p, rep, ctx], ag_s.at[p, k - 1], ag_r.at[p, k - 1],
-                    (rep, ctx_at(k), head))
-
-    def own_keep(p):
-        return pltpu.make_async_copy(own.at[p], final.at[p, rep, ctx], own_s.at[p])
-
-    def yag_copy(p, k):
-        there = final.at[p, rep, ctx_at(-k)]
-        return copy(own.at[p] if k == 0 else there, there, yag_s.at[p, k], yag_r.at[p, k],
-                    (other, ctx, head))
+    def halve_copy(p, v):
+        away = held[v].at[p, pl.ds((1 - bits[v]) * spans[v], spans[v])]
+        return copy(away, got[v].at[p], z_s.at[p, v], z_r.at[p, v], mates[v])
+
+    def double_copy(p, v):
+        mine = final.at[p, rep, pl.ds(begins[v], spans[v])]
+        return copy(mine, mine, ag_s.at[p, v], ag_r.at[p, v], mates[v])
+
+    def theirs(p, v, side):
+        first = begins[v] + (1 - 2 * bits[v]) * spans[v]
+        return final.at[p, side, pl.ds(first, spans[v])]
+
+    def yag_copy(p, v, side):
+        if v == levels:
+            there = final.at[p, side, pl.ds(begins[levels - 1], 1)]
+        else:
+            there = theirs(p, v, side)
+        return copy(there, there, yag_s.at[p, v], yag_r.at[p, v], (other, ctx, head))
 
     def h_copy(k):
         return copy(gsend.at[head_at(k)], hrecv.at[k - 1], h_s.at[k - 1], h_r.at[k - 1],
@@ -194,12 +200,10 @@
 
         def add(i):
             total = yown[p, i].astype(F32) + yrecv[p, i].astype(F32)
-            zsend[p, i] = total.astype(BF16)
+            held[0][p, i] = total.astype(BF16)
 
         each(0, n_ctx, add)
-        z_keep(p).start()
-        for k in ctx_steps:
-            z_copy(p, k).start()
+        halve_copy(p, 0).start()
 
     def attend(i):
         if groups > 2:
@@ -234,43 +238,15 @@
         gsend[:, k, :, :D_LAT] = low.reshape(n_head, own_rows, D_LAT).astype(BF16)
         gsend[:, k, :, D_LAT:] = key[:, D_LAT:].reshape(n_head, own_rows, D_ROPE).astype(BF16)
 
-    each(0, groups, attend)
-    each(0, groups, query_side)
-    for i in range(2):
-        each(i * n_ctx // 2, (i + 1) * n_ctx // 2, key_side)
-        spread(pieces - 2 + i)
-    h_keep = pltpu.make_async_copy(gsend.at[head], hrecv.at[n_head - 1], hown_s.at[0])
-    h_keep.start()
-    for k in range(1, n_head):
-        h_copy(k).start()
-
     def nope(i):
         for sub in range(PAIR):
             rows = tile(i * PAIR + sub, 128)
             d_qn[0, :, rows] = dot_tn(qlt[:D_LAT, rows], wk[:, rows]).astype(BF16)
 
-    each(0, groups, nope)
-    for m in range(groups * PAIR):
-        d_qr[0, :, m * D_ROPE:(m + 1) * D_ROPE] = qlt[D_LAT:, m * TOK:(m + 1) * TOK].T
-
-    def settle(p):
-        z_keep(p).wait()
-        total = zrecv[p, n_ctx - 1].astype(F32)
-        for k in ctx_steps:
-            z_copy(p, k).wait_recv()
-            total = total + zrecv[p, k - 1].astype(F32)
-        own[p] = total.astype(BF16)
-        for k in ctx_steps:
-            ag_copy(p, k).start()
-        yag_copy(p, 0).start()
-        own_keep(p).start()
-
-    def hand_on(p):
-        for k in ctx_steps:
-            there = final.at[p, rep, ctx_at(-k)]
-            copy(there, there, ag_s.at[p, k - 1], ag_r.at[p, k - 1],
-                 (rep, ctx_at(k), head)).wait_recv()
-            yag_copy(p, k).start()
+    def local_results():
+        each(0, groups, nope)
+        for m in range(groups * PAIR):
+            d_qr[0, :, m * D_ROPE:(m + 1) * D_ROPE] = qlt[D_LAT:, m * TOK:(m + 1) * TOK].T
 
     def latent_terms():
         h_keep.wait()
@@ -286,14 +262,69 @@
                 lsend[k - 1] = total.astype(BF16)
                 l_copy(k).start()
 
-    def settle_next(p):
-        settle(p)
-        hand_on(p - groups)
-
-    each(0, groups, settle)
-    latent_terms()
-    each(groups, pieces, settle_next)
-    each(groups, pieces, hand_on)
+    h_keep = pltpu.make_async_copy(gsend.at[head], hrecv.at[n_head - 1], hown_s.at[0])
+
+    def send_latent_terms():
+        h_keep.start()
+        for k in range(1, n_head):
+            h_copy(k).start()
+
+    def reduce_step(p, v):
+        halve_copy(p, v).wait_recv()
+
+        def add(i):
+            total = held[v][p, bits[v] * spans[v] + i].astype(F32) + got[v][p, i].astype(F32)
+            if v + 1 < levels:
+                held[v + 1][p, i] = total.astype(BF16)
+            else:
+                final[p, rep, begins[v]] = total.astype(BF16)
+
+        each(0, spans[v], add)
+        if v + 1 < levels:
+            halve_copy(p, v + 1).start()
+        else:
+            double_copy(p, v).start()
+            yag_copy(p, levels, rep).start()
+
+    def spread_step(p, v):
+        there = theirs(p, v, rep)
+        copy(there, there, ag_s.at[p, v], ag_r.at[p, v], mates[v]).wait_recv()
+        if v > 0:
+            double_copy(p, v - 1).start()
+        yag_copy(p, v, rep).start()
+
+    done = {(p, 0) for p in range(pieces - 2)}
+
+    def stage(p, at):
+        if (p, at) in done:
+            return
+        done.add((p, at))
+        if at == 0:
+            spread(p)
+        elif at <= levels:
+            reduce_step(p, at - 1)
+        else:
+            spread_step(p, 2 * levels - at)
+
+    each(0, groups, attend)
+    each(0, groups, query_side)
+    stage(0, 1)
+    stage(pieces - 2, 0)
+    stage(1, 1)
+    each(0, n_ctx // 2, key_side)
+    stage(0, 2)
+    stage(pieces - 1, 0)
+    stage(2, 1)
+    stage(1, 2)
+    each(n_ctx // 2, n_ctx, key_side)
+    send_latent_terms()
+    for wave in range(2 * levels + pieces):
+        for p in range(pieces):
+            if 0 <= wave - p <= 2 * levels:
+                stage(p, wave - p)
+        if wave == pieces:
+            local_results()
+            latent_terms()
     total = d_lat[...]
     for k in ctx_steps:
         l_copy(k).wait_recv()
@@ -309,15 +340,12 @@
 
     def end(p):
         y_copy(p).wait_send()
-        own_keep(p).wait()
-        for k in ctx_steps:
-            z_copy(p, k).wait_send()
-            ag_copy(p, k).wait_send()
-        for k in range(n_ctx):
-            there = final.at[p, other, ctx_at(-k)]
-            arrived = copy(there, there, yag_s.at[p, k], yag_r.at[p, k], (other, ctx, head))
-            arrived.wait_recv()
-            yag_copy(p, k).wait_send()
+        for v in range(levels):
+            halve_copy(p, v).wait_send()
+            double_copy(p, v).wait_send()
+        for v in range(levels + 1):
+            yag_copy(p, v, other).wait_recv()
+            yag_copy(p, v, rep).wait_send()
 
     each(0, pieces, end)
 
@@ -339,6 +367,7 @@
     rows = heads * TOK
     n_keys = n_ctx * TOK
     own = TOK // n_head
+    levels = n_ctx.bit_length() - 1
     part = (D_LAT // (2 * n_ctx), PAIR * 128)
     vmem = pl.BlockSpec(memory_space=pltpu.VMEM)
     anywhere = pl.BlockSpec(memory_space=pl.ANY)
@@ -372,9 +401,6 @@
             pltpu.VMEM((pieces, 2, n_ctx) + part, BF16),
             pltpu.VMEM((pieces, n_ctx) + part, BF16),
             pltpu.VMEM((pieces, n_ctx) + part, BF16),
-            pltpu.VMEM((pieces, n_ctx) + part, BF16),
-            pltpu.VMEM((pieces, n_ctx) + part, BF16),
-            pltpu.VMEM((pieces,) + part, BF16),
             pltpu.VMEM((n_head, n_ctx, own, WIDTH), BF16),
             pltpu.VMEM((n_head, n_ctx, own, WIDTH), BF16),
             pltpu.VMEM((n_ctx - 1, own, WIDTH), BF16),
@@ -382,13 +408,15 @@
             dma((n_ctx - 1,)), dma((n_ctx - 1,)),
             dma((n_ctx - 1,)), dma((n_ctx - 1,)),
             dma((pieces,)), dma((pieces,)),
-            dma((pieces, n_ctx - 1)), dma((pieces, n_ctx - 1)),
-            dma((pieces, n_ctx - 1)), dma((pieces, n_ctx - 1)),
-            dma((pieces, n_ctx)), dma((pieces, n_ctx)),
+            dma((pieces, levels)), dma((pieces, levels)),
+            dma((pieces, levels)), dma((pieces, levels)),
+            dma((pieces, levels + 1)), dma((pieces, levels + 1)),
             dma((n_head - 1,)), dma((n_head - 1,)),
             dma((n_ctx - 1,)), dma((n_ctx - 1,)),
-            dma((pieces,)), dma((pieces,)), dma((pieces,)), dma((1,)), dma((6,)),
-        ],
+            dma((pieces,)), dma((1,)), dma((6,)),
+        ]
+        + [pltpu.VMEM((pieces, n_ctx >> v) + part, BF16) for v in range(levels)]
+        + [pltpu.VMEM((pieces, n_ctx >> (v + 1)) + part, BF16) for v in range(levels)],
         compiler_params=pltpu.CompilerParams(
             collective_id=0, has_side_effects=True, vmem_limit_bytes=56 << 20
         ),

time: 58 us -> 58.3 us (level)
  no operation moved by 1% of the time
where the time goes in v5:
time: 58.3 us; the launch traced here: 58.1 us
  Pallas kernels  57.5 us (99%)
  between operations  0.64 us (1%)
    pallas_call x1, Pallas kernels, local(): pl.pallas_call(functools.partial(body, n_ctx, n_head, groups), out_shape=...  54.7 us
    pallas_call x1, Pallas kernels, local(): pl.pallas_call(functools.partial(finish, groups), out_shape=(jax.ShapeDty...  2.81 us

profile of v5, /device:TPU:0, one launch (start us, length us, event | category | flops | bytes accessed | tf_op | source)
XLA Modules:
  0.0 58.1 jit_solution(3239385465336851399)
XLA Ops:
  0.6 54.7 %shard_map.110 = (f32[32,576]{1,0:T(8,128)}, bf16[1,128,512]{2,1,0:T(8,128)(2,1)}, bf16[1,128,256]{2,1,0:T(8,128)(2,1)}, bf16[4,2,4,64,256]{4,3,2,1,0:T(8,128)(2,1)}) custom-call(bf16[2,288,128]{2,1,0:T(8,128)(2,1)} %bitcast.3, bf16[1,128,512]{2,1,0:T(8,128)(2,1)} %qn_in.1, bf16[1,128,256]{2,1,0:T(8,128)(2,1)} %qr_in.1, bf16[1,128,512]{2,1,0:T(8,128)(2,1)} %g_in.1, ...), custom_call_target="tpu_custom_call" | custom-call | tf_op jit(solution)/shard_map/pallas_call | solution.py:375
  55.3 2.8 %shard_map.111 = (f32[1,32,576]{2,1,0:T(8,128)}, bf16[1,128,512]{2,1,0:T(8,128)(2,1)}, bf16[1,128,256]{2,1,0:T(8,128)(2,1)}, f32[512,512]{1,0:T(8,128)}, f32[512,512]{1,0:T(8,128)}) custom-call(f32[32,576]{1,0:T(8,128)} %get-tuple-element.9.lat, bf16[1,128,512]{2,1,0:T(8,128)(2,1)} %get-tuple-element.10.qn, bf16[1,128,256]{2,1,0:T(8,128)(2,1)} %get-tuple-element.11.qr, ...), custom_call_target="tpu_custom_call" | custom-call | tf_op jit(solution)/shard_map/pallas_call | solution.py:425

commit v6 on v5

--- a/solution.py
+++ b/solution.py
@@ -53,6 +53,7 @@
     pieces = 2 * groups
     part_rows = wpart.shape[3]
     levels = n_ctx.bit_length() - 1
+    wide = groups
     held, got = held[:levels], held[levels:]
     bits = [lax.rem(ctx // (1 << v), 2) for v in range(levels)]
     mates = [(rep, ctx + (1 - 2 * bits[v]) * (1 << v), head) for v in range(levels)]
@@ -103,7 +104,8 @@
         return copy(away, got[v].at[p], z_s.at[p, v], z_r.at[p, v], mates[v])
 
     def double_copy(p, v):
-        mine = final.at[p, rep, pl.ds(begins[v], spans[v])]
+        sides = slice(0, 2) if p < wide else rep
+        mine = final.at[p, sides, pl.ds(begins[v], spans[v])]
         return copy(mine, mine, ag_s.at[p, v], ag_r.at[p, v], mates[v])
 
     def theirs(p, v, side):
@@ -283,15 +285,22 @@
         if v + 1 < levels:
             halve_copy(p, v + 1).start()
         else:
-            double_copy(p, v).start()
             yag_copy(p, levels, rep).start()
+            if p >= wide:
+                double_copy(p, v).start()
+
+    def cross_step(p):
+        if p < wide:
+            yag_copy(p, levels, other).wait_recv()
+            double_copy(p, levels - 1).start()
 
     def spread_step(p, v):
-        there = theirs(p, v, rep)
+        there = theirs(p, v, slice(0, 2) if p < wide else rep)
         copy(there, there, ag_s.at[p, v], ag_r.at[p, v], mates[v]).wait_recv()
         if v > 0:
             double_copy(p, v - 1).start()
-        yag_copy(p, v, rep).start()
+        if p >= wide:
+            yag_copy(p, v, rep).start()
 
     done = {(p, 0) for p in range(pieces - 2)}
 
@@ -303,8 +312,10 @@
             spread(p)
         elif at <= levels:
             reduce_step(p, at - 1)
+        elif at == levels + 1:
+            cross_step(p)
         else:
-            spread_step(p, 2 * levels - at)
+            spread_step(p, 2 * levels + 1 - at)
 
     each(0, groups, attend)
     each(0, groups, query_side)
@@ -318,9 +329,9 @@
     stage(1, 2)
     each(n_ctx // 2, n_ctx, key_side)
     send_latent_terms()
-    for wave in range(2 * levels + pieces):
+    for wave in range(2 * levels + 1 + pieces):
         for p in range(pieces):
-            if 0 <= wave - p <= 2 * levels:
+            if 0 <= wave - p <= 2 * levels + 1:
                 stage(p, wave - p)
         if wave == pieces:
             local_results()
@@ -343,11 +354,15 @@
         for v in range(levels):
             halve_copy(p, v).wait_send()
             double_copy(p, v).wait_send()
-        for v in range(levels + 1):
-            yag_copy(p, v, other).wait_recv()
-            yag_copy(p, v, rep).wait_send()
-
-    each(0, pieces, end)
+        yag_copy(p, levels, rep).wait_send()
+        if p >= wide:
+            yag_copy(p, levels, other).wait_recv()
+            for v in range(levels):
+                yag_copy(p, v, other).wait_recv()
+                yag_copy(p, v, rep).wait_send()
+
+    for p in range(pieces):
+        end(p)
 
 
 def finish(groups, lat, qn, qr, weights, d_lat, d_qn, d_qr, d_wk, d_wv):

time: 58.3 us -> 64.8 us (1.11)
  Pallas kernels: 57.5 us -> 63.8 us
    pallas_call x1, Pallas kernels: 54.7 us -> 61 us  [local(): pl.pallas_call(functools.partial(body, n_ctx, n_head, groups), out_shape=...]
where the time goes in v6:
time: 64.8 us; the launch traced here: 64.5 us
  Pallas kernels  63.8 us (98%)
    pallas_call x1, Pallas kernels, local(): pl.pallas_call(functools.partial(body, n_ctx, n_head, groups), out_shape=...  61 us
    pallas_call x1, Pallas kernels, local(): pl.pallas_call(functools.partial(finish, groups), out_shape=(jax.ShapeDty...  2.81 us

profile of v6, /device:TPU:0, one launch (start us, length us, event | category | flops | bytes accessed | tf_op | source)
XLA Modules:
  0.0 64.5 jit_solution(382126880660179330)
XLA Ops:
  0.6 61.0 %shard_map.110 = (f32[32,576]{1,0:T(8,128)}, bf16[1,128,512]{2,1,0:T(8,128)(2,1)}, bf16[1,128,256]{2,1,0:T(8,128)(2,1)}, bf16[4,2,4,64,256]{4,3,2,1,0:T(8,128)(2,1)}) custom-call(bf16[2,288,128]{2,1,0:T(8,128)(2,1)} %bitcast.3, bf16[1,128,512]{2,1,0:T(8,128)(2,1)} %qn_in.1, bf16[1,128,256]{2,1,0:T(8,128)(2,1)} %qr_in.1, bf16[1,128,512]{2,1,0:T(8,128)(2,1)} %g_in.1, ...), custom_call_target="tpu_custom_call" | custom-call | tf_op jit(solution)/shard_map/pallas_call | solution.py:390
  61.7 2.8 %shard_map.111 = (f32[1,32,576]{2,1,0:T(8,128)}, bf16[1,128,512]{2,1,0:T(8,128)(2,1)}, bf16[1,128,256]{2,1,0:T(8,128)(2,1)}, f32[512,512]{1,0:T(8,128)}, f32[512,512]{1,0:T(8,128)}) custom-call(f32[32,576]{1,0:T(8,128)} %get-tuple-element.9.lat, bf16[1,128,512]{2,1,0:T(8,128)(2,1)} %get-tuple-element.10.qn, bf16[1,128,256]{2,1,0:T(8,128)(2,1)} %get-tuple-element.11.qr, ...), custom_call_target="tpu_custom_call" | custom-call | tf_op jit(solution)/shard_map/pallas_call | solution.py:440

commit v7 on v4

--- a/solution.py
+++ b/solution.py
@@ -249,10 +249,6 @@
             rows = tile(i * PAIR + sub, 128)
             d_qn[0, :, rows] = dot_tn(qlt[:D_LAT, rows], wk[:, rows]).astype(BF16)
 
-    each(0, groups, nope)
-    for m in range(groups * PAIR):
-        d_qr[0, :, m * D_ROPE:(m + 1) * D_ROPE] = qlt[D_LAT:, m * TOK:(m + 1) * TOK].T
-
     def settle(p):
         z_keep(p).wait()
         total = zrecv[p, n_ctx - 1].astype(F32)
@@ -291,6 +287,9 @@
         hand_on(p - groups)
 
     each(0, groups, settle)
+    each(0, groups, nope)
+    for m in range(groups * PAIR):
+        d_qr[0, :, m * D_ROPE:(m + 1) * D_ROPE] = qlt[D_LAT:, m * TOK:(m + 1) * TOK].T
     latent_terms()
     each(groups, pieces, settle_next)
     each(groups, pieces, hand_on)

time: 58 us -> 58 us (level)
  no operation moved by 1% of the time
where the time goes in v7:
time: 58 us; the launch traced here: 57.8 us
  Pallas kernels  57.2 us (99%)
  between operations  0.64 us (1%)
    pallas_call x1, Pallas kernels, local(): pl.pallas_call(functools.partial(body, n_ctx, n_head, groups), out_shape=...  54.3 us
    pallas_call x1, Pallas kernels, local(): pl.pallas_call(functools.partial(finish, groups), out_shape=(jax.ShapeDty...  2.81 us

profile of v7, /device:TPU:0, one launch (start us, length us, event | category | flops | bytes accessed | tf_op | source)
XLA Modules:
  0.0 57.8 jit_solution(9097164647324414264)
XLA Ops:
  0.6 54.3 %shard_map.110 = (f32[32,576]{1,0:T(8,128)}, bf16[1,128,512]{2,1,0:T(8,128)(2,1)}, bf16[1,128,256]{2,1,0:T(8,128)(2,1)}, bf16[4,2,4,64,256]{4,3,2,1,0:T(8,128)(2,1)}) custom-call(bf16[2,288,128]{2,1,0:T(8,128)(2,1)} %bitcast.3, bf16[1,128,512]{2,1,0:T(8,128)(2,1)} %qn_in.1, bf16[1,128,256]{2,1,0:T(8,128)(2,1)} %qr_in.1, bf16[1,128,512]{2,1,0:T(8,128)(2,1)} %g_in.1, ...), custom_call_target="tpu_custom_call" | custom-call | tf_op jit(solution)/shard_map/pallas_call | solution.py:345
  55.0 2.8 %shard_map.111 = (f32[1,32,576]{2,1,0:T(8,128)}, bf16[1,128,512]{2,1,0:T(8,128)(2,1)}, bf16[1,128,256]{2,1,0:T(8,128)(2,1)}, f32[512,512]{1,0:T(8,128)}, f32[512,512]{1,0:T(8,128)}) custom-call(f32[32,576]{1,0:T(8,128)} %get-tuple-element.9.lat, bf16[1,128,512]{2,1,0:T(8,128)(2,1)} %get-tuple-element.10.qn, bf16[1,128,256]{2,1,0:T(8,128)(2,1)} %get-tuple-element.11.qr, ...), custom_call_target="tpu_custom_call" | custom-call | tf_op jit(solution)/shard_map/pallas_call | solution.py:396
